TPU v7x, 32 devices: a whole 2x2x4 slice. The times are simulated.
32 devices in a mesh: parts: 2 (over y), rows: 4 (over z), win: 2 (over x), rep: 2 (over core).
Axes of the slice: x: 2, y: 2, z: 4, core: 2. Of those that a mesh axis runs over, the one named last changes fastest.
Arguments:
- eig_upper: bfloat16 [196608, 2048], P(('parts', 'rows', 'rep'), 'win'), parts along dimension 0, may hold values from -0.01953125 to 0.01953125
- eig_lower: bfloat16 [196608, 2048], P(('parts', 'rows', 'rep'), 'win'), parts along dimension 0, may hold values from -6 to 6
- dipole: bfloat16 [768, 3, 256, 256], P(('parts', 'rows', 'rep')), parts along dimension 0, may hold values from -0.25 to 0.25
- block_cols: int32 [768, 3], P(('parts', 'rows', 'rep')), parts along dimension 0, may hold values from 0 to 383, as said below
- block_count: int32 [768], P(('parts', 'rows', 'rep')), parts along dimension 0, may hold values from 1 to 3, as said below
- energy_upper: float32 [4096], P(('parts', 'win')), parts along dimension 0, may hold values from 3 to 5
- energy_lower: float32 [4096], P(('parts', 'rows', 'rep')), parts along dimension 0, may hold values from 1 to 2
- sym_upper: int32 [4096], P(('parts', 'win')), parts along dimension 0, may hold values from 0 to 4
- sym_lower: int32 [4096], P(('parts', 'rows', 'rep')), parts along dimension 0, may hold values from 0 to 4
Outputs:
- einstein_a: float32 [4096, 2048], P(('parts', 'win'), ('rows', 'rep')), parts along dimension 0
- intensity: float32 [4096, 2048], P(('parts', 'win'), ('rows', 'rep')), parts along dimension 0
There are 2 independent parts, one for each index of `parts`. A program takes and returns all parts, laid end to end along the dimension named above; each array names one. Nothing has to cross between parts.
Inputs may be any that keep to these rules, and one draw needn't show every extreme that they name: `block_cols`: slot 0 of block row b names b itself; every slot names a block within 4 of its row, and some row reaches 4; a row may name a block twice. `block_count`: some block row uses all 3 slots.
All inputs are finite; a program needn't handle non-finite values.
Results may differ from a plain program's by a relative error of at most 0.0033.
Values may be sent and summed in bfloat16 or wider, within the bound.
No kernel may reach another device: no remote copies, remote signals or barrier semaphores. Data moves between devices by JAX's collectives and lax.ppermute only.
A program may use at most 320 MiB of HBM per device.

v0:
```python
import jax
import jax.numpy as jnp
from jax import lax
from jax.sharding import PartitionSpec as P

BAND = 4
JUP = 21


EMISSION = 0.3136189
RADIATION = 0.71938845


def padded_2(cells, sides, width):
    for axis, dim in sides:
        count = lax.axis_size(axis)
        ends = count - 1
        head = lax.slice_in_dim(cells, 0, width, axis=dim)
        tail = lax.slice_in_dim(cells, cells.shape[dim] - width, cells.shape[dim], axis=dim)
        cells = jnp.concatenate(
            [
                lax.ppermute(tail, axis, [(i, (i + 1) % count) for i in range(ends)]),
                cells,
                lax.ppermute(head, axis, [((i + 1) % count, i) for i in range(ends)]),
            ],
            axis=dim,
        )
    return cells


def line_values(moments, energy_upper, energy_lower, sym_upper, sym_lower):
    wavenum = energy_upper[:, None] - energy_lower[None, :]
    partner = jnp.where(sym_upper == 2, 2, jnp.where(sym_upper < 2, 1 - sym_upper, 7 - sym_upper))
    allowed = (sym_lower[None, :] == partner[:, None]).astype(jnp.float32)
    spin_weight = jnp.where(sym_upper < 2, 5.0, jnp.where(sym_upper == 2, 2.0, 3.0)).astype(
        jnp.float32
    )
    degeneracy = 2.0 * JUP + 1.0
    einstein = allowed * EMISSION * wavenum**3 * moments * moments / degeneracy
    boltzmann = jnp.exp(-RADIATION * energy_lower[None, :])
    stimulated = 1.0 - jnp.exp(-RADIATION * wavenum)
    intensity = (
        spin_weight[:, None] * degeneracy * einstein * boltzmann * stimulated / (wavenum * wavenum)
    )
    return (einstein, intensity)


def shards(
    eig_upper,
    eig_lower,
    dipole,
    block_cols,
    block_count,
    energy_upper,
    energy_lower,
    sym_upper,
    sym_lower,
):
    rows_here = dipole.shape[0]
    slot_count = dipole.shape[1]
    block_size = dipole.shape[2]
    lower_cols = eig_lower.shape[1]
    device = lax.axis_index(("rows", "rep"))
    padded = padded_2(eig_lower, ((("rows", "rep"), 0),), BAND * block_size)
    blocks = padded.reshape(rows_here + 2 * BAND, block_size, lower_cols)
    offset = device * rows_here - BAND
    where_at = block_cols - offset
    accumulated = jnp.zeros((rows_here, block_size, lower_cols), jnp.float32)
    for slot_index in range(slot_count):
        picked = jnp.take(blocks, where_at[:, slot_index], axis=0)
        product = jnp.einsum(
            "bij,bjn->bin", dipole[:, slot_index], picked, preferred_element_type=jnp.float32
        )
        live_mask = (block_count > slot_index).astype(jnp.float32)
        accumulated = accumulated + product * live_mask[:, None, None]
    lower_image = accumulated.reshape(rows_here * block_size, lower_cols).astype(jnp.bfloat16)
    partial_moments = lax.dot_general(
        eig_upper,
        lax.all_gather(lower_image, "win", axis=1, tiled=True),
        (((0,), (0,)), ((), ())),
        preferred_element_type=jnp.float32,
    )
    share = energy_lower.shape[0]
    summed = lax.psum(partial_moments, ("rows", "rep"))
    moments = lax.dynamic_slice_in_dim(summed, device * share, share, 1)
    return line_values(moments, energy_upper, energy_lower, sym_upper, sym_lower)


def solution(mesh):
    in_specs = (
        P(("parts", "rows", "rep"), "win"),
        P(("parts", "rows", "rep"), "win"),
        P(("parts", "rows", "rep"), None, None, None),
        P(("parts", "rows", "rep"), None),
        P(("parts", "rows", "rep")),
        P(("parts", "win")),
        P(("parts", "rows", "rep")),
        P(("parts", "win")),
        P(("parts", "rows", "rep")),
    )
    out_specs = (P(("parts", "win"), ("rows", "rep")), P(("parts", "win"), ("rows", "rep")))
    return jax.shard_map(shards, mesh=mesh, in_specs=in_specs, out_specs=out_specs, check_vma=False)
```

profile of v0, /device:TPU:11, one launch (start us, length us, event | category | flops | bytes accessed | tf_op | source)
XLA Modules:
  0.0 1071.6 jit_solution(10838034423047092617)
XLA Ops:
  7.2 0.0 all-gather.2.cloned.1.call-start
  7.2 4.6 fusion.28
  11.8 3.8 collective-permute-start
  15.6 1.9 collective-permute-start.1
  17.5 0.7 broadcast_subtract_fusion
  18.2 0.7 compare_convert_fusion.2
  18.9 19.9 %collective-permute-done = bf16[1024,1024]{1,0:T(8,128)(2,1)S(1)} collective-permute-done((bf16[1024,1024]{1,0:T(8,128)(2,1)}, bf16[1024,1024]{1,0:T(8,128)(2,1)S(1)}, u32[]{:S(2)}, u32[]{:S(2)}) %collective-permute-start) | collective-permute-done | bytes 2097184 | tf_op jit(solution)/shard_map/ppermute | solution.py:22
  38.9 4.4 collective-permute-done.1
  43.3 38.2 %pad_maximum_fusion = bf16[14336,1024]{1,0:T(8,128)(2,1)} fusion(bf16[1024,1024]{1,0:T(8,128)(2,1)} %collective-permute-done.1, bf16[12288,1024]{1,0:T(8,128)(2,1)} %param.12, bf16[1024,1024]{1,0:T(8,128)(2,1)S(1)} %collective-permute-done), kind=kLoop, calls=%fused_computation.4 | loop fusion | flops 88080384 | bytes 58720256 | tf_op jit(solution)/shard_map/concatenate | solution.py:20
  81.5 19.3 %gather_fusion.1 = bf16[48,256,1024]{2,1,0:T(8,128)(2,1)} fusion(bf16[56,256,1024]{2,1,0:T(8,128)(2,1)} %bitcast.35, s32[1024]{0:T(1024)S(1)} %get-tuple-element.23), kind=kCustom, calls=%fused_computation.1.clone | custom fusion | bytes 50331840 | tf_op jit(solution)/shard_map/jit(_take)/gather | solution.py:70
  100.8 19.3 %gather_fusion.2 = bf16[48,256,1024]{2,1,0:T(8,128)(2,1)} fusion(bf16[56,256,1024]{2,1,0:T(8,128)(2,1)} %bitcast.36, s32[1024]{0:T(1024)S(1)} %get-tuple-element.22), kind=kCustom, calls=%fused_computation.2.clone | custom fusion | bytes 50331840 | tf_op jit(solution)/shard_map/jit(_take)/gather | solution.py:70
  120.1 19.2 %gather_fusion = bf16[48,256,1024]{2,1,0:T(8,128)(2,1)} fusion(bf16[56,256,1024]{2,1,0:T(8,128)(2,1)} %bitcast.37, s32[1024]{0:T(1024)S(1)} %pad_clamp_fusion.2), kind=kCustom, calls=%fused_computation.clone | custom fusion | bytes 50331840 | tf_op jit(solution)/shard_map/jit(_take)/gather | solution.py:70
  139.3 27.5 %fusion.2 = f32[48,1024,256]{1,2,0:T(8,128)} fusion(bf16[48,256,1024]{2,1,0:T(8,128)(2,1)} %gather_fusion.1, pred[48]{0:T(512)(128)(4,1)S(1)} %get-tuple-element.15, bf16[48,3,256,256]{3,2,1,0:T(8,128)(2,1)} %param.13), kind=kOutput, calls=%fused_computation.7 | convolution fusion | flops 6455033856 | bytes 81788976 | tf_op jit(solution)/shard_map/bij,bjn->bin/dot_general | solution.py:71
  166.8 27.3 %fusion.4 = f32[48,1024,256]{1,2,0:T(8,128)} fusion(bf16[48,256,1024]{2,1,0:T(8,128)(2,1)} %gather_fusion, pred[48]{0:T(512)(128)(4,1)S(1)} %get-tuple-element.17, bf16[48,3,256,256]{3,2,1,0:T(8,128)(2,1)} %param.13), kind=kOutput, calls=%fused_computation.9 | convolution fusion | flops 6455033856 | bytes 81788976 | tf_op jit(solution)/shard_map/bij,bjn->bin/dot_general | solution.py:71
  194.1 50.9 %add_convert_fusion = bf16[48,1024,256]{1,2,0:T(8,128)(2,1)} fusion(f32[48,1024,256]{1,2,0:T(8,128)} %fusion.2, f32[48,1024,256]{1,2,0:T(8,128)} %fusion.4, f32[48]{0:T(128)S(1)} %get-tuple-element.20, f32[48]{0:T(128)S(1)} %get-tuple-element.21, f32[48]{0:T(128)S(1)} %get-tuple-element.19, bf16[48,256,1024]{2,1,0:T(8,128)(2,1)} %gather_fusion.2, ...), kind=kOutput, calls=%fused_computation.3 | convolution fusion | flops 6530531328 | bytes 157287024 | tf_op jit(solution)/shard_map/bij,bjn->bin/dot_general | solution.py:71
  245.0 0.0 all-gather.2.cloned.1.call-update
  245.0 0.0 copy-start.2
  245.0 0.0 copy-start
  245.0 0.0 copy-start.1
  245.1 0.0 copy-start.3
  245.1 0.2 all-reduce.2.cloned.1.call-start
  245.3 576.8 %all-gather.2.cloned.1.call-done = bf16[12288,2048]{1,0:T(8,128)(2,1)} async-done(((bf16[12288,1024]{1,0:T(8,128)(2,1)}), bf16[12288,2048]{1,0:T(8,128)(2,1)}) %all-gather.2.cloned.1.call-update) | async-done | bytes 50331664 | tf_op jit(solution)/shard_map/all_gather | solution.py:79
  822.1 61.6 %convolution_bitcast_fusion = f32[1024,2048]{0,1:T(8,128)} fusion(bf16[12288,2048]{1,0:T(8,128)(2,1)} %all-gather.2.cloned.1.call-done, bf16[12288,1024]{1,0:T(8,128)(2,1)} %param.11), kind=kOutput, calls=%fused_computation.23 | convolution fusion | flops 51539607552 | bytes 83886080 | tf_op jit(solution)/shard_map/dot_general | solution.py:77
  883.7 0.0 all-reduce.2.cloned.1.call-update
  883.7 0.0 copy-done.2
  883.8 0.0 copy-done
  883.8 176.4 %all-reduce.2.cloned.1.call-done = f32[1024,2048]{0,1:T(8,128)} async-done(((f32[1024,2048]{0,1:T(8,128)}), f32[1024,2048]{0,1:T(8,128)}) %all-reduce.2.cloned.1.call-update) | async-done | bytes 8388624 | tf_op jit(solution)/shard_map/psum | solution.py:84
  1060.2 0.0 copy-done.1
  1060.2 0.0 copy-done.3
  1060.2 2.0 fusion.20
  1062.2 1.3 copy.14
  1063.5 1.3 copy.15
  (6 shorter events, 0.0 us)
Async XLA Ops:
  7.2 815.0 %all-gather.2.cloned.1.call-start = ((), (), s32[]{:S(2)}) async-start(), calls=%async_computation | async-start | bytes 75497472 | tf_op jit(solution)/shard_map/all_gather | solution.py:79
  11.8 27.0 %collective-permute-start = (bf16[1024,1024]{1,0:T(8,128)(2,1)}, bf16[1024,1024]{1,0:T(8,128)(2,1)S(1)}, u32[]{:S(2)}, u32[]{:S(2)}) collective-permute-start(bf16[1024,1024]{1,0:T(8,128)(2,1)} %get-tuple-element.11), channel_id=1, source_target_pairs={{0,1},{1,4},{4,5},{5,8},{8,9},{9,12},{12,13},{2,3},{3,6},{6,7},{7,... | collective-permute-start | bytes 6291464 | tf_op jit(solution)/shard_map/ppermute | solution.py:22
  15.6 27.7 %collective-permute-start.1 = (bf16[1024,1024]{1,0:T(8,128)(2,1)}, bf16[1024,1024]{1,0:T(8,128)(2,1)}, u32[]{:S(2)}, u32[]{:S(2)}) collective-permute-start(bf16[1024,1024]{1,0:T(8,128)(2,1)} %get-tuple-element.12), channel_id=1, source_target_pairs={{1,0},{4,1},{5,4},{8,5},{9,8},{12,9},{13,12},{3,2},{6,3},{7,6},{10... | collective-permute-start | bytes 6291464 | tf_op jit(solution)/shard_map/ppermute | solution.py:24
  245.0 638.7 %copy-start.2 = (f32[256]{0:T(256)S(1)}, f32[256]{0:T(256)}, u32[]{:S(2)}) copy-start(f32[256]{0:T(256)} %param.17) | copy-start | bytes 3076
  245.0 638.7 %copy-start = (s32[1024]{0:T(1024)S(1)}, s32[1024]{0:T(1024)}, u32[]{:S(2)}) copy-start(s32[1024]{0:T(1024)} %param.18) | copy-start | bytes 12292
  245.0 815.2 %copy-start.1 = (f32[1024]{0:T(1024)S(1)}, f32[1024]{0:T(1024)}, u32[]{:S(2)}) copy-start(f32[1024]{0:T(1024)} %param.16) | copy-start | bytes 12292
  245.1 815.2 %copy-start.3 = (s32[256]{0:T(256)S(1)}, s32[256]{0:T(256)}, u32[]{:S(2)}) copy-start(s32[256]{0:T(256)} %param.19) | copy-start | bytes 3076
  245.1 815.2 %all-reduce.2.cloned.1.call-start = ((), (), s32[]{:S(2)}) async-start(), calls=%async_computation.1 | async-start | bytes 16777216 | tf_op jit(solution)/shard_map/psum | solution.py:84
Sparse Core Ops, SparseCore 0:
  245.1 576.9 all-gather.1
  883.9 176.3 all-reduce.1
where the time goes:
time: 1070 us
  waiting for transfers between devices  778 us (73%)
  matrix products  167 us (16%)
  local copies, waits for them, and re-layouts  65.1 us (6%)
  other arithmetic  41.6 us (4%)
  between operations  14.2 us (1%)
    all_gather x1, waiting for transfers between devices, shards(): lax.all_gather(lower_image, 'win', axis=1, tiled=True)  577 us
    psum x1, waiting for transfers between devices, shards(): summed = lax.psum(partial_moments, ('rows', 'rep'))  176 us
    dot_general x3, matrix products, shards(): jnp.einsum('bij,bjn->bin', dipole[:, slot_index], picked, preferred_eleme...  106 us
    dot_general x1, matrix products, shards(): lax.dot_general(eig_upper, lax.all_gather(lower_image, 'win', axis=1, til...  61.6 us
    gather x3, local copies, waits for them, and re-layouts, shards(): picked = jnp.take(blocks, where_at[:, slot_index], axis=0)  57.8 us
    concatenate x1, other arithmetic, padded_2(): jnp.concatenate([lax.ppermute(tail, axis, [(i, (i + 1) % count) for i in...  38.2 us
  transfers between devices with their start and end apart: 4, of which 4 were waited for; matrix products, arithmetic and copies ran while one was open for 0% of the time, Pallas kernels for 0%

commit v1 on v0

v1 whole, which is shorter than its diff:
```python
import functools

import jax
import jax.numpy as jnp
from jax import lax
from jax.experimental import pallas as pl
from jax.experimental.pallas import tpu as pltpu
from jax.sharding import PartitionSpec as P

BAND = 4
JUP = 21


EMISSION = 0.3136189
RADIATION = 0.71938845
LANES = 128
TAIL = 2


def line_values(moments, energy_upper, energy_lower, sym_upper, sym_lower):
    wavenum = energy_upper[:, None] - energy_lower[None, :]
    partner = jnp.where(sym_upper == 2, 2, jnp.where(sym_upper < 2, 1 - sym_upper, 7 - sym_upper))
    allowed = (sym_lower[None, :] == partner[:, None]).astype(jnp.float32)
    spin_weight = jnp.where(sym_upper < 2, 5.0, jnp.where(sym_upper == 2, 2.0, 3.0)).astype(
        jnp.float32
    )
    degeneracy = 2.0 * JUP + 1.0
    einstein = allowed * EMISSION * wavenum**3 * moments * moments / degeneracy
    boltzmann = jnp.exp(-RADIATION * energy_lower[None, :])
    stimulated = 1.0 - jnp.exp(-RADIATION * wavenum)
    intensity = (
        spin_weight[:, None] * degeneracy * einstein * boltzmann * stimulated / (wavenum * wavenum)
    )
    return (einstein, intensity)


def image_kernel(slots, starts, where_ref, count_ref, turn_ref, dipole_ref, *refs):
    sources = refs[: 1 + 3 * (slots - 1)]
    outs, acc = refs[len(sources) : -1], refs[-1]
    row = pl.program_id(0)
    rows_here = pl.num_programs(0)
    acc[...] = jnp.dot(dipole_ref[0, 0], sources[0][...], preferred_element_type=jnp.float32)
    for slot in range(1, slots):
        place = where_ref[row * slots + slot]
        live = count_ref[row] > slot
        own, low, high = sources[1 + 3 * (slot - 1) : 4 + 3 * (slot - 1)]
        low_side, high_side = place < 0, place >= rows_here

        def add(ref, slot=slot):
            acc[...] += jnp.dot(dipole_ref[0, slot], ref[...], preferred_element_type=jnp.float32)

        pl.when(live & low_side)(functools.partial(add, low))
        pl.when(live & high_side)(functools.partial(add, high))
        pl.when(live & jnp.logical_not(low_side | high_side))(functools.partial(add, own))
    outs[0][...] = acc[...].astype(jnp.bfloat16)
    cols = acc.shape[1]
    for out, start in zip(outs[1:], starts):
        at = lax.rem(turn_ref[0] + start, cols)
        out[...] = outs[0][:, pl.ds(pl.multiple_of(at, LANES), LANES)]


def image(where_at, block_count, turn, dipole, lower, low, high, starts):
    rows_here, slots, size = dipole.shape[:3]
    cols = lower.shape[1]

    def at(slot, first, blocks):
        def index(row, where_ref, count_ref, turn_ref):
            return jnp.clip(where_ref[row * slots + slot] - first, 0, blocks - 1), 0

        return pl.BlockSpec((size, cols), index)

    by_row = lambda row, *_: (row, 0)
    specs = [
        pl.BlockSpec((1, slots, size, size), lambda row, *_: (row, 0, 0, 0)),
        pl.BlockSpec((size, cols), by_row),
    ]
    operands = [dipole, lower]
    for slot in range(1, slots):
        specs += [at(slot, 0, rows_here), at(slot, -BAND, BAND), at(slot, rows_here, BAND)]
        operands += [lower, low, high]
    out_specs = [pl.BlockSpec((size, cols), by_row)] + [pl.BlockSpec((size, LANES), by_row)] * len(starts)
    out_shape = [jax.ShapeDtypeStruct(lower.shape, jnp.bfloat16)] + [
        jax.ShapeDtypeStruct((lower.shape[0], LANES), jnp.bfloat16)
    ] * len(starts)
    return pl.pallas_call(
        functools.partial(image_kernel, slots, starts),
        grid_spec=pltpu.PrefetchScalarGridSpec(
            num_scalar_prefetch=3,
            grid=(rows_here,),
            in_specs=specs,
            out_specs=out_specs,
            scratch_shapes=[pltpu.VMEM((size, cols), jnp.float32)],
        ),
        out_shape=out_shape,
        compiler_params=pltpu.CompilerParams(vmem_limit_bytes=40 * 2**20),
        cost_estimate=pl.CostEstimate(
            flops=2 * rows_here * slots * size * size * cols,
            bytes_accessed=2 * rows_here * slots * size * (size + cols) + 4 * lower.size,
            transcendentals=0,
        ),
    )(where_at.reshape(-1), block_count, turn, *operands)


def halo(lower, width, axes):
    count = 1
    for axis in axes:
        count *= lax.axis_size(axis)
    up = [(i, i + 1) for i in range(count - 1)]
    down = [(i + 1, i) for i in range(count - 1)]
    low = lax.ppermute(lower[-width:], axes, up)
    high = lax.ppermute(lower[:width], axes, down)
    return low, high


def product(chunk, eig_upper):
    return lax.dot_general(
        chunk, eig_upper, (((0,), (0,)), ((), ())), preferred_element_type=jnp.float32
    )


def to_owner(partial, owner, rows, wins, reps):
    half = partial.shape[1] // reps
    rep = lax.axis_index("rep")
    mine = lax.dynamic_slice_in_dim(partial, rep * half, half, 1)
    for turn in range(1, reps):
        out = lax.dynamic_slice_in_dim(partial, (rep + turn) % reps * half, half, 1)
        mine = mine + lax.ppermute(out, "rep", [(i, (i + turn) % reps) for i in range(reps)])
    axes = ("rows", "win", "rep")
    place = lambda row, win, part: (row * wins + win) * reps + part
    pieces = []
    me = place(lax.axis_index("rows"), lax.axis_index("win"), rep)
    for part in range(reps):
        keep = functools.reduce(
            jnp.logical_or,
            [me == place(*owner(win)[:1], win, part) for win in range(wins) if owner(win)[1] == part],
            jnp.bool_(False),
        )
        total = jnp.where(keep, mine, 0.0)
        for turn in range(rows):
            pairs = []
            for win in range(wins):
                row, core = owner(win)
                if turn or core != part:
                    pairs.append((place((row + turn) % rows, win, part), place(row, win, core)))
            if pairs:
                total = total + lax.ppermute(mine, axes, pairs)
        pieces.append(total)
    return jnp.concatenate(pieces, axis=1)


def shards(
    eig_upper,
    eig_lower,
    dipole,
    block_cols,
    block_count,
    energy_upper,
    energy_lower,
    sym_upper,
    sym_lower,
):
    rows_here = dipole.shape[0]
    block_size = dipole.shape[2]
    cols = eig_lower.shape[1]
    share = energy_lower.shape[0]
    rows, wins, reps = (lax.axis_size(axis) for axis in ("rows", "win", "rep"))
    owners = ("rows", "rep")
    device = lax.axis_index(owners)
    win = lax.axis_index("win")
    chunks = cols // LANES
    tail = TAIL if wins == 2 and share == TAIL * LANES else 0
    turn_of = lambda w: (w * 2 // wins) * (cols // 2)

    where_at = block_cols - device * rows_here
    turn = turn_of(win)
    first = lax.dynamic_slice_in_dim(eig_lower, turn, LANES, 1)
    raw = [
        lax.ppermute(first, "win", [(i, (i + step) % wins) for i in range(wins)]) for step in range(1, wins)
    ]
    low, high = halo(eig_lower, BAND * block_size, owners)
    starts = tuple(LANES * i for i in range(1, chunks))
    whole, *sent = image(
        where_at, block_count, turn[None], dipole, eig_lower, low, high, starts
    )
    partials = jnp.zeros((cols * wins, eig_upper.shape[1]), jnp.float32)
    partials = lax.dynamic_update_slice_in_dim(partials, product(whole, eig_upper), win * cols, 0)
    late = []
    none = jnp.zeros((1,), jnp.int32)
    for step in range(1, wins):
        source = (win - step) % wins
        pairs = [(i, (i + step) % wins) for i in range(wins)]
        for index in range(chunks):
            if index:
                got = lax.ppermute(sent[index - 1], "win", pairs)
            else:
                ends = halo(raw[step - 1], BAND * block_size, owners)
                (got,) = image(where_at, block_count, none, dipole, raw[step - 1], *ends, ())
            part = product(got, eig_upper)
            if index < chunks - tail:
                at = source * cols + (turn_of(source) + index * LANES) % cols
                partials = lax.dynamic_update_slice_in_dim(partials, part, at, 0)
            else:

                def owner(w):
                    source = (w - step) % wins
                    at = source * cols + (turn_of(source) + index * LANES) % cols
                    return divmod(at // share, reps)

                late.append(to_owner(part, owner, rows, wins, reps))
    moments = lax.psum_scatter(partials, owners, scatter_dimension=0, tiled=True)
    if late:
        moments = moments + jnp.concatenate(late, axis=0)
    return line_values(moments.T, energy_upper, energy_lower, sym_upper, sym_lower)


def solution(mesh):
    in_specs = (
        P(("parts", "rows", "rep"), "win"),
        P(("parts", "rows", "rep"), "win"),
        P(("parts", "rows", "rep"), None, None, None),
        P(("parts", "rows", "rep"), None),
        P(("parts", "rows", "rep")),
        P(("parts", "win")),
        P(("parts", "rows", "rep")),
        P(("parts", "win")),
        P(("parts", "rows", "rep")),
    )
    out_specs = (P(("parts", "win"), ("rows", "rep")), P(("parts", "win"), ("rows", "rep")))
    return jax.shard_map(shards, mesh=mesh, in_specs=in_specs, out_specs=out_specs, check_vma=False)
```

time: 1070 us -> 661 us (0.62)
  waiting for transfers between devices: 778 us -> 354 us
  Pallas kernels: 0 us -> 106 us
  matrix products: 167 us -> 117 us
  other arithmetic: 41.6 us -> 2.54 us
  local copies, waits for them, and re-layouts: 65.1 us -> 31.4 us
  starting transfers between devices: 5.93 us -> 34.5 us
    all_gather x1 -> x0, waiting for transfers between devices: 577 us -> none  [shards(): lax.all_gather(lower_image, 'win', axis=1, tiled=True)]
    ppermute x2 -> x28, waiting for transfers between devices: 24.3 us -> 354 us  [the longest x7 314 us: shards(): got = lax.ppermute(sent[index - 1], 'win', pairs)]
    psum x1 -> x0, waiting for transfers between devices: 176 us -> none  [shards(): summed = lax.psum(partial_moments, ('rows', 'rep'))]
    pallas_call x0 -> x2, Pallas kernels: none -> 106 us  [image(): pl.pallas_call(functools.partial(image_kernel, slots, starts), grid_spec=...]
    gather x3 -> x0, local copies, waits for them, and re-layouts: 57.8 us -> none  [shards(): picked = jnp.take(blocks, where_at[:, slot_index], axis=0)]
    dot_general x4 -> x9, matrix products: 167 us -> 117 us  [product(): lax.dot_general(chunk, eig_upper, (((0,), (0,)), ((), ())), preferred_ele...]
    concatenate x1 -> x0, other arithmetic: 38.2 us -> none  [padded_2(): jnp.concatenate([lax.ppermute(tail, axis, [(i, (i + 1) % count) for i in...]
    ppermute x2 -> x28, starting transfers between devices: 5.67 us -> 34.4 us  [the longest x14 18.1 us: to_owner(): total = total + lax.ppermute(mine, axes, pairs)]
  transfers between devices with their start and end apart: 4 -> 29, of which waited for: 4 -> 11; matrix products, arithmetic and copies ran while one was open for 0% -> 19% of each run, Pallas kernels for 0% -> 16%
where the time goes in v1:
time: 661 us; the launch traced here: 660 us
  waiting for transfers between devices  354 us (54%)
  matrix products  117 us (18%)
  Pallas kernels  106 us (16%)
  starting transfers between devices  34.5 us (5%)
  local copies, waits for them, and re-layouts  31.4 us (5%)
  between operations  14.6 us (2%)
    ppermute x7, waiting for transfers between devices, shards(): got = lax.ppermute(sent[index - 1], 'win', pairs)  314 us
    dot_general x9, matrix products, product(): lax.dot_general(chunk, eig_upper, (((0,), (0,)), ((), ())), preferred_ele...  117 us
    pallas_call x2, Pallas kernels, image(): pl.pallas_call(functools.partial(image_kernel, slots, starts), grid_spec=...  106 us
    ppermute x14, waiting for transfers between devices, to_owner(): total = total + lax.ppermute(mine, axes, pairs)  18.5 us
    ppermute x14, starting transfers between devices, to_owner(): total = total + lax.ppermute(mine, axes, pairs)  18.1 us
    ppermute x2, waiting for transfers between devices, halo(): low = lax.ppermute(lower[-width:], axes, up)  17.6 us
    dynamic_update_slice x6, local copies, waits for them, and re-layouts, shards(): partials = lax.dynamic_update_slice_in_dim(partials, part, at, 0)  17.6 us
  transfers between devices with their start and end apart: 29, of which 11 were waited for; matrix products, arithmetic and copies ran while one was open for 19% of the time, Pallas kernels for 16%

profile of v1, /device:TPU:11, one launch (start us, length us, event | category | flops | bytes accessed | tf_op | source)
XLA Modules:
  0.0 659.9 jit_solution(2708741372913819172)
XLA Ops:
  7.2 4.6 fusion.6
  11.9 3.8 collective-permute-start
  17.6 3.2 constant_dynamic-slice_fusion.2
  21.3 17.6 %collective-permute-done.refs_2_.refs_5_ = bf16[1024,1024]{1,0:T(8,128)(2,1)} collective-permute-done((bf16[1024,1024]{1,0:T(8,128)(2,1)}, bf16[1024,1024]{1,0:T(8,128)(2,1)}, u32[]{:S(2)}, u32[]{:S(2)}) %collective-permute-start) | collective-permute-done | bytes 2097184 | tf_op jit(solution)/shard_map/ppermute | solution.py:110
  38.9 4.6 collective-permute-done.1.refs_3_.refs_6_
  43.5 69.9 %shard_map.104 = (bf16[12288,1024]{1,0:T(8,128)(2,1)}, bf16[12288,128]{1,0:T(8,128)(2,1)}, bf16[12288,128]{1,0:T(8,128)(2,1)}, bf16[12288,128]{1,0:T(8,128)(2,1)...) custom-call(s32[144]{0:T(256)S(1)} %reshape.17.where_ref, ...), custom_call_target="tpu_custom_call" | custom-call | flops 19327352832 | bytes 144703488 | tf_op jit(solution)/shard_map/pallas_call | solution.py:85
  117.1 2.6 collective-permute-start.4
  120.8 31.2 %convolution_dynamic-update-slice_fusion = f32[2048,1024]{1,0:T(8,128)S(1)} fusion(f32[2048,1024]{1,0:T(8,128)S(1)} %broadcast_in_dim.33, s32[]{:T(128)S(6)} %select_n.116, bf16[12288,1024]{1,0:T(8,128)(2,1)} %get-tuple-element.10, bf16[12288,1024]{1,0:T(8,128)(2,1)} %param.9), kind=kOutput, calls=%fused_computation | convolution fusion | flops 25769803776 | bytes 54525956 | tf_op jit(solution)/shard_map/dot_general | solution.py:116
  156.5 35.7 %shard_map.105 = bf16[12288,128]{1,0:T(8,128)(2,1)S(1)} custom-call(s32[144]{0:T(256)S(1)} %reshape.17.where_ref, s32[48]{0:T(128)S(1)} %copy-done, s32[1]{0:T(128)} %constant.124.clone.1.turn_ref, bf16[48,3,256,256]{3,2,1,0:T(8,128)(2,1)} %dipole_ref.3, bf16[12288,128]{1,0:T(8,128)(2,1)S(1)} %collective-permute-done.2.refs_0_.refs_1_.refs_4_, ...), custom_call_target="tpu_custom_call" | custom-call | flops 2415919104 | bytes 34603008 | tf_op jit(solution)/shard_map/pallas_call | solution.py:85
  192.2 10.0 %fusion.8 = f32[128,1024]{1,0:T(8,128)S(1)} fusion(bf16[12288,128]{1,0:T(8,128)(2,1)S(1)} %shard_map.105, bf16[12288,1024]{1,0:T(8,128)(2,1)} %param.9), kind=kOutput, calls=%fused_computation.30 | convolution fusion | flops 3221225472 | bytes 28835840 | tf_op jit(solution)/shard_map/dot_general | solution.py:116
  202.2 2.9 dynamic_update_slice.22
  205.2 10.9 %fusion.9 = f32[128,1024]{1,0:T(8,128)S(1)} fusion(bf16[12288,128]{1,0:T(8,128)(2,1)} %collective-permute-done.5, bf16[12288,1024]{1,0:T(8,128)(2,1)} %param.9), kind=kOutput, calls=%fused_computation.31 | convolution fusion | flops 3221225472 | bytes 28835840 | tf_op jit(solution)/shard_map/dot_general | solution.py:116
  216.1 35.3 %collective-permute-done.6 = bf16[12288,128]{1,0:T(8,128)(2,1)} collective-permute-done((bf16[12288,128]{1,0:T(8,128)(2,1)}, bf16[12288,128]{1,0:T(8,128)(2,1)}, u32[]{:S(2)}, u32[]{:S(2)}) %collective-permute-start.6) | collective-permute-done | bytes 3145760 | tf_op jit(solution)/shard_map/ppermute | solution.py:194
  251.3 10.9 %fusion.10 = f32[128,1024]{1,0:T(8,128)S(1)} fusion(bf16[12288,128]{1,0:T(8,128)(2,1)} %collective-permute-done.6, bf16[12288,1024]{1,0:T(8,128)(2,1)} %param.9), kind=kOutput, calls=%fused_computation.32 | convolution fusion | flops 3221225472 | bytes 28835840 | tf_op jit(solution)/shard_map/dot_general | solution.py:116
  262.3 56.5 %collective-permute-done.7 = bf16[12288,128]{1,0:T(8,128)(2,1)} collective-permute-done((bf16[12288,128]{1,0:T(8,128)(2,1)}, bf16[12288,128]{1,0:T(8,128)(2,1)}, u32[]{:S(2)}, u32[]{:S(2)}) %collective-permute-start.7) | collective-permute-done | bytes 3145760 | tf_op jit(solution)/shard_map/ppermute | solution.py:194
  318.7 10.9 %fusion.11 = f32[128,1024]{1,0:T(8,128)S(1)} fusion(bf16[12288,128]{1,0:T(8,128)(2,1)} %collective-permute-done.7, bf16[12288,1024]{1,0:T(8,128)(2,1)} %param.9), kind=kOutput, calls=%fused_computation.33 | convolution fusion | flops 3221225472 | bytes 28835840 | tf_op jit(solution)/shard_map/dot_general | solution.py:116
  329.7 2.9 dynamic_update_slice.23
  332.6 2.9 dynamic_update_slice.24
  335.5 2.9 dynamic_update_slice.25
  338.4 47.7 %collective-permute-done.8 = bf16[12288,128]{1,0:T(8,128)(2,1)} collective-permute-done((bf16[12288,128]{1,0:T(8,128)(2,1)}, bf16[12288,128]{1,0:T(8,128)(2,1)}, u32[]{:S(2)}, u32[]{:S(2)}) %collective-permute-start.8) | collective-permute-done | bytes 3145760 | tf_op jit(solution)/shard_map/ppermute | solution.py:194
  386.2 10.9 %fusion.12 = f32[128,1024]{1,0:T(8,128)S(1)} fusion(bf16[12288,128]{1,0:T(8,128)(2,1)} %collective-permute-done.8, bf16[12288,1024]{1,0:T(8,128)(2,1)} %param.9), kind=kOutput, calls=%fused_computation.34 | convolution fusion | flops 3221225472 | bytes 28835840 | tf_op jit(solution)/shard_map/dot_general | solution.py:116
  397.1 2.9 dynamic_update_slice.26
  400.0 50.8 %collective-permute-done.9 = bf16[12288,128]{1,0:T(8,128)(2,1)} collective-permute-done((bf16[12288,128]{1,0:T(8,128)(2,1)}, bf16[12288,128]{1,0:T(8,128)(2,1)}, u32[]{:S(2)}, u32[]{:S(2)}) %collective-permute-start.9) | collective-permute-done | bytes 3145760 | tf_op jit(solution)/shard_map/ppermute | solution.py:194
  450.8 10.9 %fusion.13 = f32[128,1024]{1,0:T(8,128)S(1)} fusion(bf16[12288,128]{1,0:T(8,128)(2,1)} %collective-permute-done.9, bf16[12288,1024]{1,0:T(8,128)(2,1)} %param.9), kind=kOutput, calls=%fused_computation.35 | convolution fusion | flops 3221225472 | bytes 28835840 | tf_op jit(solution)/shard_map/dot_general | solution.py:116
  461.7 2.9 dynamic_update_slice.27
  466.2 69.0 %collective-permute-done.10 = bf16[12288,128]{1,0:T(8,128)(2,1)} collective-permute-done((bf16[12288,128]{1,0:T(8,128)(2,1)}, bf16[12288,128]{1,0:T(8,128)(2,1)}, u32[]{:S(2)}, u32[]{:S(2)}) %collective-permute-start.10) | collective-permute-done | bytes 3145760 | tf_op jit(solution)/shard_map/ppermute | solution.py:194
  535.2 11.1 %fusion.14 = f32[128,1024]{1,0:T(8,128)S(1)} fusion(bf16[12288,128]{1,0:T(8,128)(2,1)} %collective-permute-done.10, bf16[12288,1024]{1,0:T(8,128)(2,1)} %param.9), kind=kOutput, calls=%fused_computation.36 | convolution fusion | flops 3221225472 | bytes 28835840 | tf_op jit(solution)/shard_map/dot_general | solution.py:116
  546.5 54.4 %collective-permute-done.19 = bf16[12288,128]{1,0:T(8,128)(2,1)S(1)} collective-permute-done((bf16[12288,128]{1,0:T(8,128)(2,1)}, bf16[12288,128]{1,0:T(8,128)(2,1)S(1)}, u32[]{:S(2)}, u32[]{:S(2)}) %collective-permute-start.19) | collective-permute-done | bytes 3145760 | tf_op jit(solution)/shard_map/ppermute | solution.py:194
  600.9 10.0 %fusion.15 = f32[128,1024]{1,0:T(8,128)S(1)} fusion(bf16[12288,128]{1,0:T(8,128)(2,1)S(1)} %collective-permute-done.19, bf16[12288,1024]{1,0:T(8,128)(2,1)} %param.9), kind=kOutput, calls=%fused_computation.37 | convolution fusion | flops 3221225472 | bytes 28835840 | tf_op jit(solution)/shard_map/dot_general | solution.py:116
  619.0 8.8 %collective-permute-done.13 = f32[128,512]{1,0:T(8,128)S(1)} collective-permute-done((f32[128,512]{1,0:T(8,128)S(1)}, f32[128,512]{1,0:T(8,128)S(1)}, u32[]{:S(2)}, u32[]{:S(2)}) %collective-permute-start.13) | collective-permute-done | bytes 262176 | tf_op jit(solution)/shard_map/ppermute | solution.py:146
  634.5 3.2 collective-permute-done.25
  641.9 6.4 collective-permute-done.22
  (80 shorter events, 36.8 us)
Async XLA Ops:
  7.2 641.2 %reduce-scatter.2.cloned.1.call-start = ((), (), s32[]{:S(2)}) async-start(), calls=%async_computation.1 | async-start | bytes 9437184 | tf_op jit(solution)/shard_map/reduce_scatter | solution.py:210
  11.9 27.0 %collective-permute-start = (bf16[1024,1024]{1,0:T(8,128)(2,1)}, bf16[1024,1024]{1,0:T(8,128)(2,1)}, u32[]{:S(2)}, u32[]{:S(2)}) collective-permute-start(bf16[1024,1024]{1,0:T(8,128)(2,1)} %get-tuple-element.25), channel_id=1, source_target_pairs={{0,1},{1,4},{4,5},{5,8},{8,9},{9,12},{12,13},{2,3},{3,6},{6,7},{7,... | collective-permute-start | bytes 6291464 | tf_op jit(solution)/shard_map/ppermute | solution.py:110
  15.6 27.9 %collective-permute-start.1 = (bf16[1024,1024]{1,0:T(8,128)(2,1)}, bf16[1024,1024]{1,0:T(8,128)(2,1)}, u32[]{:S(2)}, u32[]{:S(2)}) collective-permute-start(bf16[1024,1024]{1,0:T(8,128)(2,1)} %get-tuple-element.24), channel_id=1, source_target_pairs={{1,0},{4,1},{5,4},{8,5},{9,8},{12,9},{13,12},{3,2},{6,3},{7,6},{10... | collective-permute-start | bytes 6291464 | tf_op jit(solution)/shard_map/ppermute | solution.py:111
  20.8 94.3 %collective-permute-start.2 = (bf16[12288,128]{1,0:T(8,128)(2,1)}, bf16[12288,128]{1,0:T(8,128)(2,1)S(1)}, u32[]{:S(2)}, u32[]{:S(2)}) collective-permute-start(bf16[12288,128]{1,0:T(8,128)(2,1)} %constant_dynamic-slice_fusion.2), channel_id=1, source_target_pairs={{0,2},{2,0},{1,3},{3,1},{4,6},{6,4},{5,7},{7,5},{8,10},{10,8},{9,1... | collective-permute-start | bytes 9437192 | tf_op jit(solution)/shard_map/ppermute | solution.py:178
  113.4 91.8 %collective-permute-start.5 = (bf16[12288,128]{1,0:T(8,128)(2,1)}, bf16[12288,128]{1,0:T(8,128)(2,1)}, u32[]{:S(2)}, u32[]{:S(2)}) collective-permute-start(bf16[12288,128]{1,0:T(8,128)(2,1)} %get-tuple-element.11), channel_id=1, source_target_pairs={{0,2},{2,0},{1,3},{3,1},{4,6},{6,4},{5,7},{7,5},{8,10},{10,8},{9,1... | collective-permute-start | bytes 9437192 | tf_op jit(solution)/shard_map/ppermute | solution.py:194
  113.7 137.7 %collective-permute-start.6 = (bf16[12288,128]{1,0:T(8,128)(2,1)}, bf16[12288,128]{1,0:T(8,128)(2,1)}, u32[]{:S(2)}, u32[]{:S(2)}) collective-permute-start(bf16[12288,128]{1,0:T(8,128)(2,1)} %get-tuple-element.12), channel_id=1, source_target_pairs={{0,2},{2,0},{1,3},{3,1},{4,6},{6,4},{5,7},{7,5},{8,10},{10,8},{9,1... | collective-permute-start | bytes 9437192 | tf_op jit(solution)/shard_map/ppermute | solution.py:194
  114.9 203.9 %collective-permute-start.7 = (bf16[12288,128]{1,0:T(8,128)(2,1)}, bf16[12288,128]{1,0:T(8,128)(2,1)}, u32[]{:S(2)}, u32[]{:S(2)}) collective-permute-start(bf16[12288,128]{1,0:T(8,128)(2,1)} %get-tuple-element.13), channel_id=1, source_target_pairs={{0,2},{2,0},{1,3},{3,1},{4,6},{6,4},{5,7},{7,5},{8,10},{10,8},{9,1... | collective-permute-start | bytes 9437192 | tf_op jit(solution)/shard_map/ppermute | solution.py:194
  115.2 36.8 %collective-permute-start.3 = (bf16[1024,128]{1,0:T(8,128)(2,1)S(1)}, bf16[1024,128]{1,0:T(8,128)(2,1)S(1)}, u32[]{:S(2)}, u32[]{:S(2)}) collective-permute-start(bf16[1024,128]{1,0:T(8,128)(2,1)S(1)} %get-tuple-element.27), channel_id=1, source_target_pairs={{0,1},{1,4},{4,5},{5,8},{8,9},{9,12},{12,13},{2,3},{3,6},{6,7},{7,... | collective-permute-start | bytes 786440 | tf_op jit(solution)/shard_map/ppermute | solution.py:110
  117.1 36.2 %collective-permute-start.4 = (bf16[1024,128]{1,0:T(8,128)(2,1)S(1)}, bf16[1024,128]{1,0:T(8,128)(2,1)S(1)}, u32[]{:S(2)}, u32[]{:S(2)}) collective-permute-start(bf16[1024,128]{1,0:T(8,128)(2,1)S(1)} %get-tuple-element.26), channel_id=1, source_target_pairs={{1,0},{4,1},{5,4},{8,5},{9,8},{12,9},{13,12},{3,2},{6,3},{7,6},{10... | collective-permute-start | bytes 786440 | tf_op jit(solution)/shard_map/ppermute | solution.py:111
  152.0 234.1 %collective-permute-start.8 = (bf16[12288,128]{1,0:T(8,128)(2,1)}, bf16[12288,128]{1,0:T(8,128)(2,1)}, u32[]{:S(2)}, u32[]{:S(2)}) collective-permute-start(bf16[12288,128]{1,0:T(8,128)(2,1)} %get-tuple-element.14), channel_id=1, source_target_pairs={{0,2},{2,0},{1,3},{3,1},{4,6},{6,4},{5,7},{7,5},{8,10},{10,8},{9,1... | collective-permute-start | bytes 9437192 | tf_op jit(solution)/shard_map/ppermute | solution.py:194
  155.3 295.5 %collective-permute-start.9 = (bf16[12288,128]{1,0:T(8,128)(2,1)}, bf16[12288,128]{1,0:T(8,128)(2,1)}, u32[]{:S(2)}, u32[]{:S(2)}) collective-permute-start(bf16[12288,128]{1,0:T(8,128)(2,1)} %get-tuple-element.15), channel_id=1, source_target_pairs={{0,2},{2,0},{1,3},{3,1},{4,6},{6,4},{5,7},{7,5},{8,10},{10,8},{9,1... | collective-permute-start | bytes 9437192 | tf_op jit(solution)/shard_map/ppermute | solution.py:194
  464.7 70.5 %collective-permute-start.10 = (bf16[12288,128]{1,0:T(8,128)(2,1)}, bf16[12288,128]{1,0:T(8,128)(2,1)}, u32[]{:S(2)}, u32[]{:S(2)}) collective-permute-start(bf16[12288,128]{1,0:T(8,128)(2,1)} %get-tuple-element.16), channel_id=1, source_target_pairs={{0,2},{2,0},{1,3},{3,1},{4,6},{6,4},{5,7},{7,5},{8,10},{10,8},{9,1... | collective-permute-start | bytes 9437192 | tf_op jit(solution)/shard_map/ppermute | solution.py:194
  465.0 135.9 %collective-permute-start.19 = (bf16[12288,128]{1,0:T(8,128)(2,1)}, bf16[12288,128]{1,0:T(8,128)(2,1)S(1)}, u32[]{:S(2)}, u32[]{:S(2)}) collective-permute-start(bf16[12288,128]{1,0:T(8,128)(2,1)} %get-tuple-element.17), channel_id=1, source_target_pairs={{0,2},{2,0},{1,3},{3,1},{4,6},{6,4},{5,7},{7,5},{8,10},{10,8},{9,1... | collective-permute-start | bytes 9437192 | tf_op jit(solution)/shard_map/ppermute | solution.py:194
  546.4 85.4 %copy-start.4 = (f32[256]{0:T(256)S(1)}, f32[256]{0:T(256)}, u32[]{:S(2)}) copy-start(f32[256]{0:T(256)} %param.15) | copy-start | bytes 3076
  546.4 64.6 %collective-permute-start.11 = (f32[128,512]{1,0:T(8,128)S(1)}, f32[128,512]{1,0:T(8,128)S(1)}, u32[]{:S(2)}, u32[]{:S(2)}) collective-permute-start(f32[128,512]{1,0:T(8,128)S(1)} %constant_dynamic-slice_fusion.1), channel_id=1, source_target_pairs={{0,1},{1,0},{2,3},{3,2},{4,5},{5,4},{6,7},{7,6},{8,9},{9,8},{10,11... | collective-permute-start | bytes 786440 | tf_op jit(solution)/shard_map/ppermute | solution.py:127
  610.9 5.4 collective-permute-start.20
  611.1 37.3 %copy-start.3 = (f32[1024]{0:T(1024)S(1)}, f32[1024]{0:T(1024)}, u32[]{:S(2)}) copy-start(f32[1024]{0:T(1024)} %param.14) | copy-start | bytes 12292
  611.1 37.3 %copy-start.6 = (s32[256]{0:T(256)S(1)}, s32[256]{0:T(256)}, u32[]{:S(2)}) copy-start(s32[256]{0:T(256)} %param.17) | copy-start | bytes 3076
  611.1 6.6 collective-permute-start.12
  612.4 15.4 %collective-permute-start.13 = (f32[128,512]{1,0:T(8,128)S(1)}, f32[128,512]{1,0:T(8,128)S(1)}, u32[]{:S(2)}, u32[]{:S(2)}) collective-permute-start(f32[128,512]{1,0:T(8,128)S(1)} %dynamic-slice_add_fusion.1), channel_id=1, source_target_pairs={{12,9},{10,7},{28,25},{26,23}} | collective-permute-start | bytes 786440 | tf_op jit(solution)/shard_map/ppermute | solution.py:146
  613.7 15.4 %collective-permute-start.16 = (f32[128,512]{1,0:T(8,128)S(1)}, f32[128,512]{1,0:T(8,128)S(1)}, u32[]{:S(2)}, u32[]{:S(2)}) collective-permute-start(f32[128,512]{1,0:T(8,128)S(1)} %dynamic-slice_add_fusion.1), channel_id=1, source_target_pairs={{13,9},{11,7},{29,25},{27,23}} | collective-permute-start | bytes 786440 | tf_op jit(solution)/shard_map/ppermute | solution.py:146
  615.0 15.4 %collective-permute-start.17 = (f32[128,512]{1,0:T(8,128)S(1)}, f32[128,512]{1,0:T(8,128)S(1)}, u32[]{:S(2)}, u32[]{:S(2)}) collective-permute-start(f32[128,512]{1,0:T(8,128)S(1)} %dynamic-slice_add_fusion.1), channel_id=1, source_target_pairs={{1,9},{15,7},{17,25},{31,23}} | collective-permute-start | bytes 786440 | tf_op jit(solution)/shard_map/ppermute | solution.py:146
  616.3 15.5 %collective-permute-start.18 = (f32[128,512]{1,0:T(8,128)S(1)}, f32[128,512]{1,0:T(8,128)S(1)}, u32[]{:S(2)}, u32[]{:S(2)}) collective-permute-start(f32[128,512]{1,0:T(8,128)S(1)} %dynamic-slice_add_fusion.1), channel_id=1, source_target_pairs={{5,9},{3,7},{21,25},{19,23}} | collective-permute-start | bytes 786440 | tf_op jit(solution)/shard_map/ppermute | solution.py:146
  617.7 15.5 %collective-permute-start.14 = (f32[128,512]{1,0:T(8,128)S(1)}, f32[128,512]{1,0:T(8,128)S(1)}, u32[]{:S(2)}, u32[]{:S(2)}) collective-permute-start(f32[128,512]{1,0:T(8,128)S(1)} %dynamic-slice_add_fusion.1), channel_id=1, source_target_pairs={{0,9},{14,7},{16,25},{30,23}} | collective-permute-start | bytes 786440 | tf_op jit(solution)/shard_map/ppermute | solution.py:146
  627.8 9.9 %collective-permute-start.25 = (f32[128,512]{1,0:T(8,128)S(1)}, f32[128,512]{1,0:T(8,128)S(1)}, u32[]{:S(2)}, u32[]{:S(2)}) collective-permute-start(f32[128,512]{1,0:T(8,128)S(1)} %dynamic-slice_add_fusion), channel_id=1, source_target_pairs={{13,9},{11,7},{29,25},{27,23}} | collective-permute-start | bytes 786440 | tf_op jit(solution)/shard_map/ppermute | solution.py:146
  629.1 9.9 %collective-permute-start.26 = (f32[128,512]{1,0:T(8,128)S(1)}, f32[128,512]{1,0:T(8,128)S(1)}, u32[]{:S(2)}, u32[]{:S(2)}) collective-permute-start(f32[128,512]{1,0:T(8,128)S(1)} %dynamic-slice_add_fusion), channel_id=1, source_target_pairs={{1,9},{15,7},{17,25},{31,23}} | collective-permute-start | bytes 786440 | tf_op jit(solution)/shard_map/ppermute | solution.py:146
  630.4 9.9 %collective-permute-start.27 = (f32[128,512]{1,0:T(8,128)S(1)}, f32[128,512]{1,0:T(8,128)S(1)}, u32[]{:S(2)}, u32[]{:S(2)}) collective-permute-start(f32[128,512]{1,0:T(8,128)S(1)} %dynamic-slice_add_fusion), channel_id=1, source_target_pairs={{5,9},{3,7},{21,25},{19,23}} | collective-permute-start | bytes 786440 | tf_op jit(solution)/shard_map/ppermute | solution.py:146
  631.8 10.0 %collective-permute-start.15 = (f32[128,512]{1,0:T(8,128)S(1)}, f32[128,512]{1,0:T(8,128)S(1)}, u32[]{:S(2)}, u32[]{:S(2)}) collective-permute-start(f32[128,512]{1,0:T(8,128)S(1)} %dynamic-slice_add_fusion.1), channel_id=1, source_target_pairs={{4,9},{2,7},{20,25},{18,23}} | collective-permute-start | bytes 786440 | tf_op jit(solution)/shard_map/ppermute | solution.py:146
  633.2 8.7 %collective-permute-start.21 = (f32[128,512]{1,0:T(8,128)S(1)}, f32[128,512]{1,0:T(8,128)S(1)}, u32[]{:S(2)}, u32[]{:S(2)}) collective-permute-start(f32[128,512]{1,0:T(8,128)S(1)} %dynamic-slice_add_fusion), channel_id=1, source_target_pairs={{8,9},{6,7},{24,25},{22,23}} | collective-permute-start | bytes 786440 | tf_op jit(solution)/shard_map/ppermute | solution.py:146
  637.7 10.5 %collective-permute-start.22 = (f32[128,512]{1,0:T(8,128)S(1)}, f32[128,512]{1,0:T(8,128)S(1)}, u32[]{:S(2)}, u32[]{:S(2)}) collective-permute-start(f32[128,512]{1,0:T(8,128)S(1)} %dynamic-slice_add_fusion), channel_id=1, source_target_pairs={{12,9},{10,7},{28,25},{26,23}} | collective-permute-start | bytes 786440 | tf_op jit(solution)/shard_map/ppermute | solution.py:146
  639.0 9.2 %collective-permute-start.23 = (f32[128,512]{1,0:T(8,128)S(1)}, f32[128,512]{1,0:T(8,128)S(1)}, u32[]{:S(2)}, u32[]{:S(2)}) collective-permute-start(f32[128,512]{1,0:T(8,128)S(1)} %dynamic-slice_add_fusion), channel_id=1, source_target_pairs={{0,9},{14,7},{16,25},{30,23}} | collective-permute-start | bytes 786440 | tf_op jit(solution)/shard_map/ppermute | solution.py:146
  640.3 7.9 %collective-permute-start.24 = (f32[128,512]{1,0:T(8,128)S(1)}, f32[128,512]{1,0:T(8,128)S(1)}, u32[]{:S(2)}, u32[]{:S(2)}) collective-permute-start(f32[128,512]{1,0:T(8,128)S(1)} %dynamic-slice_add_fusion), channel_id=1, source_target_pairs={{4,9},{2,7},{20,25},{18,23}} | collective-permute-start | bytes 786440 | tf_op jit(solution)/shard_map/ppermute | solution.py:146
  (4 other events, 34.2 us)
Sparse Core Ops, SparseCore 0:
  464.8 85.8 reduce-scatter.1

commit v2 on v1

v2 whole, which is shorter than its diff:
```python
import functools

import jax
import jax.numpy as jnp
from jax import lax
from jax.experimental import pallas as pl
from jax.experimental.pallas import tpu as pltpu
from jax.sharding import PartitionSpec as P

BAND = 4
JUP = 21


EMISSION = 0.3136189
RADIATION = 0.71938845
LANES = 128
AXES = ("rows", "win", "rep")
VMEM = 60 * 2**20
SMALL = pl.CostEstimate(flops=1024, bytes_accessed=1024, transcendentals=0)


def image_kernel(slots, pieces, where_ref, count_ref, turn_ref, dipole_ref, *refs):
    sources = refs[: 1 + 3 * (slots - 1)]
    outs, acc = refs[len(sources) : -1], refs[-1]
    row = pl.program_id(0)
    rows_here = pl.num_programs(0)
    acc[...] = jnp.dot(dipole_ref[0, 0], sources[0][...], preferred_element_type=jnp.float32)
    for slot in range(1, slots):
        place = where_ref[row * slots + slot]
        live = count_ref[row] > slot
        own, low, high = sources[1 + 3 * (slot - 1) : 4 + 3 * (slot - 1)]
        low_side, high_side = place < 0, place >= rows_here

        def add(ref, slot=slot):
            acc[...] += jnp.dot(dipole_ref[0, slot], ref[...], preferred_element_type=jnp.float32)

        pl.when(live & low_side)(functools.partial(add, low))
        pl.when(live & high_side)(functools.partial(add, high))
        pl.when(live & jnp.logical_not(low_side | high_side))(functools.partial(add, own))
    outs[0][...] = acc[...].astype(jnp.bfloat16)
    cols = acc.shape[1]
    half = LANES // 2

    def tile(start):
        at = lax.rem(turn_ref[0] + start // LANES * LANES, cols)
        return acc[:, pl.ds(pl.multiple_of(at, LANES), LANES)]

    for out, (tiles, top, bottom) in zip(outs[1:], pieces):

        @pl.when((row >= top) & (row < bottom))
        def _(out=out, tiles=tiles):
            for index, starts in enumerate(tiles):
                value = tile(starts[0])
                if len(starts) > 1:
                    left = lax.broadcasted_iota(jnp.int32, value.shape, 1) < half
                    other = tile(starts[1])
                    if starts[0] % LANES:
                        value = pltpu.roll(value, half, 1)
                    else:
                        other = pltpu.roll(other, half, 1)
                    value = jnp.where(left, value, other)
                out[:, index * LANES : (index + 1) * LANES] = value.astype(jnp.bfloat16)


def image(where_at, block_count, turn, dipole, lower, low, high, pieces):
    rows_here, slots, size = dipole.shape[:3]
    cols = lower.shape[1]

    def at(slot, first, blocks):
        def index(row, where_ref, count_ref, turn_ref):
            return jnp.clip(where_ref[row * slots + slot] - first, 0, blocks - 1), 0

        return pl.BlockSpec((size, cols), index)

    by_row = lambda row, *_: (row, 0)
    specs = [
        pl.BlockSpec((1, slots, size, size), lambda row, *_: (row, 0, 0, 0)),
        pl.BlockSpec((size, cols), by_row),
    ]
    operands = [dipole, lower]
    for slot in range(1, slots):
        specs += [at(slot, 0, rows_here), at(slot, -BAND, BAND), at(slot, rows_here, BAND)]
        operands += [lower, low, high]
    out_specs = [pl.BlockSpec((size, cols), by_row)]
    out_shape = [jax.ShapeDtypeStruct(lower.shape, jnp.bfloat16)]
    for tiles, top, bottom in pieces:
        width = LANES * len(tiles)
        out_specs.append(
            pl.BlockSpec(
                (size, width),
                lambda row, *_, top=top, bottom=bottom: (jnp.clip(row, top, bottom - 1) - top, 0),
            )
        )
        out_shape.append(jax.ShapeDtypeStruct(((bottom - top) * size, width), jnp.bfloat16))
    return pl.pallas_call(
        functools.partial(image_kernel, slots, pieces),
        grid_spec=pltpu.PrefetchScalarGridSpec(
            num_scalar_prefetch=3,
            grid=(rows_here,),
            in_specs=specs,
            out_specs=out_specs,
            scratch_shapes=[pltpu.VMEM((size, cols), jnp.float32)],
        ),
        out_shape=out_shape,
        compiler_params=pltpu.CompilerParams(vmem_limit_bytes=VMEM),
        cost_estimate=SMALL,
    )(where_at.reshape(-1), block_count, turn, *operands)


def product_kernel(chunk_ref, upper_ref, out):
    @pl.when(pl.program_id(0) == 0)
    def _():
        out[...] = jnp.zeros_like(out)

    out[...] += lax.dot_general(
        chunk_ref[...], upper_ref[...], (((0,), (0,)), ((), ())), preferred_element_type=jnp.float32
    )


def product(chunk, eig_upper):
    depth, width = chunk.shape
    uppers = eig_upper.shape[1]
    step = 1024
    while depth % step:
        step //= 2
    return pl.pallas_call(
        product_kernel,
        grid=(depth // step,),
        in_specs=[pl.BlockSpec((step, width), lambda i: (i, 0)), pl.BlockSpec((step, uppers), lambda i: (i, 0))],
        out_specs=pl.BlockSpec((width, uppers), lambda i: (0, 0)),
        out_shape=jax.ShapeDtypeStruct((width, uppers), jnp.float32),
        compiler_params=pltpu.CompilerParams(vmem_limit_bytes=VMEM),
        cost_estimate=SMALL,
    )(chunk, eig_upper)


def part_product(chunk, eig_upper, first, given):
    part = lax.dot_general(
        chunk,
        eig_upper[first : first + chunk.shape[0]],
        (((0,), (0,)), ((), ())),
        preferred_element_type=jnp.float32,
    )
    return part if given is None else given + part


def lines_kernel(late, given, energy_upper, energy_lower, sym_upper, sym_lower, moments_ref, *refs):
    einstein_out, intensity_out = refs[-2:]
    moments = moments_ref[...]
    if late:
        parts = refs[given : given + late]
        total = parts[0][...].astype(jnp.float32)
        for part in parts[1:]:
            total = total + part[...].astype(jnp.float32)
        first = moments.shape[0] - total.shape[0]
        moments = jnp.concatenate([moments[:first], moments[first:] + total], axis=0)
    moments = moments.T
    label = sym_upper[...]
    partner = jnp.where(label == 2, 2, jnp.where(label < 2, 1 - label, 7 - label)).astype(jnp.float32)
    spin_weight = jnp.where(label < 2, 5.0, jnp.where(label == 2, 2.0, 3.0)).astype(jnp.float32)
    spread = lambda row: jnp.broadcast_to(row, (8, row.shape[1])).T[:, :1]
    upper, partner, spin_weight = spread(energy_upper[...]), spread(partner), spread(spin_weight)
    lower, other = energy_lower[...], sym_lower[...].astype(jnp.float32)
    wavenum = upper - lower
    degeneracy = 2.0 * JUP + 1.0
    strength = jnp.where(other == partner, EMISSION / degeneracy, 0.0) * (moments * moments) * wavenum
    boltzmann = jnp.exp(-RADIATION * lower)
    stimulated = 1.0 - jnp.exp(-RADIATION * wavenum)
    einstein_out[...] = strength * (wavenum * wavenum)
    intensity_out[...] = strength * (spin_weight * degeneracy) * (boltzmann * stimulated)


def lines(moments, late, first, count, outs, energy_upper, energy_lower, sym_upper, sym_lower):
    shape = (energy_upper.shape[0], energy_lower.shape[0])
    at = first // count
    full = lambda array: pl.BlockSpec(array.shape, lambda i: (0, 0))
    column = lambda height: pl.BlockSpec((height, count), lambda i: (0, at))
    operands = [energy_upper[None, :], energy_lower[None, :], sym_upper[None, :], sym_lower[None, :], moments]
    specs = [full(operands[0]), column(1), full(operands[2]), column(1)]
    specs += [full(moments)]
    specs += [pl.BlockSpec(memory_space=pl.ANY)] * len(outs) + [full(part) for part in late]
    return pl.pallas_call(
        functools.partial(lines_kernel, len(late), len(outs)),
        grid=(1,),
        in_specs=specs,
        out_specs=[column(shape[0])] * 2,
        out_shape=[jax.ShapeDtypeStruct(shape, jnp.float32)] * 2,
        input_output_aliases={len(operands) + i: i for i in range(len(outs))},
        compiler_params=pltpu.CompilerParams(vmem_limit_bytes=VMEM),
    )(*operands, *outs, *late)


def copy_kernel(at_ref, array_ref, out):
    out[...] = array_ref[...]


def columns(array, at, width):
    step = array.shape[0] // 6
    return pl.pallas_call(
        copy_kernel,
        grid_spec=pltpu.PrefetchScalarGridSpec(
            num_scalar_prefetch=1,
            grid=(6,),
            in_specs=[pl.BlockSpec((step, width), lambda i, at_ref: (i, at_ref[0]))],
            out_specs=pl.BlockSpec((step, width), lambda i, at_ref: (i, 0)),
        ),
        out_shape=jax.ShapeDtypeStruct((array.shape[0], width), array.dtype),
        compiler_params=pltpu.CompilerParams(vmem_limit_bytes=VMEM),
        cost_estimate=SMALL,
    )(at[None], array)


def halo(last, first, axes):
    count = 1
    for axis in axes:
        count *= lax.axis_size(axis)
    up = [(i, i + 1) for i in range(count - 1)]
    down = [(i + 1, i) for i in range(count - 1)]
    low = lax.ppermute(last, axes, up)
    high = lax.ppermute(first, axes, down)
    return low, high


def place(row, win, core):
    return (row * lax.axis_size("win") + win) * lax.axis_size("rep") + core


def to_chips(partial, groups, chip, wire=jnp.float32):
    rows, wins, reps = (lax.axis_size(axis) for axis in AXES)
    row, win, rep = (lax.axis_index(axis) for axis in AXES)
    split = partial.reshape(groups, reps, -1, partial.shape[1])
    of_core = lambda core: lax.dynamic_index_in_dim(split, core, 1, keepdims=False)
    mine = of_core(rep)
    for turn in range(1, reps):
        pairs = [(i, (i + turn) % reps) for i in range(reps)]
        mine = mine + lax.ppermute(of_core((rep + turn) % reps), "rep", pairs)
    first = functools.reduce(lambda at, w: jnp.where(win == w, chip(w), at), range(1, wins), chip(0))
    terms = []
    sent = mine.astype(wire)
    for turn in [*range(rows - 1, 0, -1), 0]:
        at = (row - turn - first) % rows
        piece = lax.dynamic_index_in_dim(sent if turn else mine, jnp.minimum(at, groups - 1), 0, keepdims=False)
        if turn:
            pairs = [
                (place((chip(w) + g + turn) % rows, w, core), place(chip(w) + g, w, core))
                for w in range(wins)
                for g in range(groups)
                for core in range(reps)
            ]
            terms.append(lax.ppermute(piece, AXES, pairs))
        else:
            terms.append(jnp.where(at < groups, piece, 0.0))
    return terms


def shards(
    eig_upper,
    eig_lower,
    dipole,
    block_cols,
    block_count,
    energy_upper,
    energy_lower,
    sym_upper,
    sym_lower,
):
    rows_here = dipole.shape[0]
    size = dipole.shape[2]
    cols = eig_lower.shape[1]
    depth = eig_lower.shape[0]
    uppers = eig_upper.shape[1]
    share = energy_lower.shape[0]
    rows, wins, reps = (lax.axis_size(axis) for axis in AXES)
    owners = ("rows", "rep")
    device = lax.axis_index(owners)
    row, win, rep = (lax.axis_index(axis) for axis in AXES)
    group = reps * share
    groups = cols // group
    chunks = group // LANES
    shift = lambda w: (w * 2 // wins) * (groups // 2)
    turn = shift(win) * group

    where_at = block_cols - device * rows_here
    none = jnp.zeros((1,), jnp.int32)
    raws = min(2, chunks)
    width = BAND * size
    first = columns(eig_lower, turn // (raws * LANES), raws * LANES)
    behind, first = lax.optimization_barrier((eig_lower, first))
    low, high = halo(behind[-width:], behind[:width], owners)

    tail = LANES // 2 if wins == 2 and reps == 2 and share == 2 * LANES else 0
    plan = [("raw", 0, (), 0, rows_here, (0, share) if raws == chunks else None)]
    for g in range(groups):
        start, end = g * group + (raws * LANES if g == 0 else 0), (g + 1) * group
        if tail and g == groups - 1:
            at = [start + core * share for core in range(reps)]
            plan.append(("whole", g, tuple((i,) for i in at), 0, rows_here, (0, LANES)))
            plan.append(("whole", g, (tuple(i + LANES for i in at),), 0, rows_here, (LANES, tail)))
            cuts = [0, rows_here * 5 // 8, rows_here * 7 // 8, rows_here]
            for top, bottom in zip(cuts, cuts[1:]):
                plan.append(("cut", g, (tuple(i + LANES + tail for i in at),), top, bottom, None))
            continue
        for at in range(start, end, 2 * LANES):
            tiles = tuple((i,) for i in range(at, min(at + 2 * LANES, end), LANES))
            plan.append(("whole", g, tiles, 0, rows_here, None))
        if start < end:
            plan[-1] = (*plan[-1][:-1], (0, share))
    whole, *sent = image(
        where_at, block_count, turn[None], dipole, eig_lower, low, high, tuple(item[2:5] for item in plan[1:])
    )
    own = product(whole, eig_upper)
    transfers = [
        (step, *item, array) for step in range(1, wins) for item, array in zip(plan, [first, *sent])
    ]
    count = len(transfers)
    got, late, waiting = [], [], []
    sums = {}
    summed = lambda last: [total for _, at, total in sums.values() if at <= last]

    def collect(part, groups, chip, when, start):
        terms = to_chips(part, groups, chip)
        sums[len(sums)] = start, when, functools.reduce(jnp.add, terms)

    def work(index, after):
        step, kind, g, _, top, bottom, batch, _ = transfers[index]
        piece, after, waiting[:] = lax.optimization_barrier((got[index], after, list(waiting)))

        def chip(w):
            source = (w - step) % wins
            return source * groups + (g + shift(source)) % groups

        if kind == "cut":
            part = part_product(piece, eig_upper, top * size, waiting.pop() if waiting else None)
            if bottom < rows_here:
                waiting.append(part)
            else:
                late.extend(to_chips(part, 1, chip, jnp.bfloat16))
            return part
        if kind == "raw":
            ends = halo(piece[-width:], piece[:width], owners)
            (piece,) = image(where_at, block_count, none, dipole, piece, *ends, ())
        part = product(piece, eig_upper)
        waiting.append(part)
        if batch:
            collect(jnp.concatenate(waiting, axis=0), 1, chip, index, batch[0])
            waiting.clear()
        return part

    def moments_of(first, many):
        total = jnp.zeros((many, uppers), jnp.float32)
        for start, _, term in sums.values():
            end = start + term.shape[0]
            low_end, high_end = max(start, first), min(end, first + many)
            if low_end < high_end:
                term = term[low_end - start : high_end - start]
                total = total + jnp.pad(term, ((low_end - first, first + many - high_end), (0, 0)))
        return total

    levels = (energy_upper, energy_lower, sym_upper, sym_lower)
    outs, rest = [], None
    for index in range(count + 2):
        ready = index - 2
        if ready == 0:
            collect(own, groups, lambda w: w * groups, 0, 0)
        if ready >= 0:
            after = summed(ready - 1) if ready > 1 else [own]
            if tail and ready == count - 2:
                outs = lines(moments_of(0, LANES), [], 0, LANES, [], *levels)
                rest = moments_of(LANES, LANES)
                after += [rest, *outs]
            made = work(ready, after)
        if index < count:
            step, *_, array = transfers[index]
            if ready >= 0:
                needs = got[ready] if transfers[ready][1] == "cut" else (got[ready], made)
                array, _ = lax.optimization_barrier((array, needs))
            got.append(lax.ppermute(array, "win", [(i, (i + step) % wins) for i in range(wins)]))
    if not tail:
        return tuple(lines(moments_of(0, share), [], 0, share, [], *levels))
    return tuple(lines(rest, late, LANES, LANES, outs, *levels))


def solution(mesh):
    in_specs = (
        P(("parts", "rows", "rep"), "win"),
        P(("parts", "rows", "rep"), "win"),
        P(("parts", "rows", "rep"), None, None, None),
        P(("parts", "rows", "rep"), None),
        P(("parts", "rows", "rep")),
        P(("parts", "win")),
        P(("parts", "rows", "rep")),
        P(("parts", "win")),
        P(("parts", "rows", "rep")),
    )
    out_specs = (P(("parts", "win"), ("rows", "rep")), P(("parts", "win"), ("rows", "rep")))
    return jax.shard_map(shards, mesh=mesh, in_specs=in_specs, out_specs=out_specs, check_vma=False)
```

time: 661 us -> 577 us (0.87)
  Pallas kernels: 106 us -> 219 us
  matrix products: 117 us -> 13.8 us
  waiting for transfers between devices: 354 us -> 261 us
  local copies, waits for them, and re-layouts: 31.4 us -> 12.5 us
  starting transfers between devices: 34.5 us -> 50.4 us
  between operations: 14.6 us -> 1.08 us
  other arithmetic: 2.54 us -> 15.3 us
    pallas_call x2 -> x10, Pallas kernels: 106 us -> 219 us  [the longest x2 104 us: image(): pl.pallas_call(functools.partial(image_kernel, slots, pieces), grid_spec=...]
    dot_general x9 -> x3, matrix products: 117 us -> 13.8 us  [part_product(): lax.dot_general(chunk, eig_upper[first:first + chunk.shape[0]], (((0,), (...]
    ppermute x28 -> x31, waiting for transfers between devices: 354 us -> 261 us  [the longest x15 145 us: to_chips(): terms.append(lax.ppermute(piece, AXES, pairs))]
    dynamic_update_slice x6 -> x0, local copies, waits for them, and re-layouts: 17.6 us -> none  [shards(): partials = lax.dynamic_update_slice_in_dim(partials, part, at, 0)]
    ppermute x28 -> x31, starting transfers between devices: 34.4 us -> 50.4 us  [the longest x15 25.5 us: to_chips(): terms.append(lax.ppermute(piece, AXES, pairs))]
    add x6 -> x8, other arithmetic: 0.47 us -> 9.88 us  [the longest x3 4.62 us: collect(): sums[len(sums)] = (start, when, functools.reduce(jnp.add, terms))]
  transfers between devices with their start and end apart: 29 -> 31, of which waited for: 11 -> 24; matrix products, arithmetic and copies ran while one was open for 19% -> 6% of each run, Pallas kernels for 16% -> 36%
where the time goes in v2:
time: 577 us; the launch traced here: 573 us
  waiting for transfers between devices  261 us (45%)
  Pallas kernels  219 us (38%)
  starting transfers between devices  50.4 us (9%)
  other arithmetic  15.3 us (3%)
  matrix products  13.8 us (2%)
  local copies, waits for them, and re-layouts  12.5 us (2%)
    ppermute x15, waiting for transfers between devices, to_chips(): terms.append(lax.ppermute(piece, AXES, pairs))  145 us
    pallas_call x2, Pallas kernels, image(): pl.pallas_call(functools.partial(image_kernel, slots, pieces), grid_spec=...  104 us
    pallas_call x5, Pallas kernels, product(): pl.pallas_call(product_kernel, grid=(depth // step,), in_specs=[pl.BlockS...  101 us
    ppermute x7, waiting for transfers between devices, shards(): lax.ppermute(array, 'win', [(i, (i + step) % wins) for i in range(wins)])  77.6 us
    ppermute x15, starting transfers between devices, to_chips(): terms.append(lax.ppermute(piece, AXES, pairs))  25.5 us
    ppermute x2, waiting for transfers between devices, halo(): low = lax.ppermute(last, axes, up)  24.7 us
    dot_general x3, matrix products, part_product(): lax.dot_general(chunk, eig_upper[first:first + chunk.shape[0]], (((0,), (...  13.8 us
  transfers between devices with their start and end apart: 31, of which 24 were waited for; matrix products, arithmetic and copies ran while one was open for 6% of the time, Pallas kernels for 36%

profile of v2, /device:TPU:11, one launch (start us, length us, event | category | flops | bytes accessed | tf_op | source)
XLA Modules:
  0.0 572.7 jit_solution(4436140340918424559)
XLA Ops:
  0.7 6.9 %shard_map.104 = bf16[12288,256]{1,0:T(8,128)(2,1)} custom-call(s32[1]{0:T(128)} %bitcast.5.at_ref, bf16[12288,1024]{1,0:T(8,128)(2,1)} %refs_4_.1), custom_call_target="tpu_custom_call" | custom-call | flops 1024 | bytes 1024 | tf_op jit(solution)/shard_map/pallas_call | solution.py:199
  7.8 4.7 fusion.11
  12.6 4.0 collective-permute-start
  19.4 20.5 %collective-permute-done.refs_2_.refs_5_ = bf16[1024,1024]{1,0:T(8,128)(2,1)S(1)} collective-permute-done((bf16[1024,1024]{1,0:T(8,128)(2,1)}, bf16[1024,1024]{1,0:T(8,128)(2,1)S(1)}, u32[]{:S(2)}, u32[]{:S(2)}) %collective-permute-start) | collective-permute-done | bytes 2097184 | tf_op jit(solution)/shard_map/ppermute | solution.py:219
  39.9 4.7 collective-permute-done.1.refs_3_.refs_6_
  44.6 66.3 %shard_map.105 = (bf16[12288,1024]{1,0:T(8,128)(2,1)}, bf16[12288,256]{1,0:T(8,128)(2,1)}, bf16[12288,256]{1,0:T(8,128)(2,1)}, bf16[12288,128]{1,0:T(8,128)(2,1)...) custom-call(s32[144]{0:T(256)} %reshape.29.where_ref, s32[48]{0:T(128)} %count_ref.3, ...), custom_call_target="tpu_custom_call" | custom-call | flops 1024 | bytes 1024 | tf_op jit(solution)/shard_map/pallas_call | solution.py:95
  112.2 33.1 %shard_map.106 = f32[1024,1024]{1,0:T(8,128)} custom-call(bf16[12288,1024]{1,0:T(8,128)(2,1)} %get-tuple-element.29.chunk_ref, bf16[12288,1024]{1,0:T(8,128)(2,1)} %upper_ref.9), custom_call_target="tpu_custom_call" | custom-call | flops 1024 | bytes 1024 | tf_op jit(solution)/shard_map/pallas_call | solution.py:126
  146.6 4.7 collective-permute-start.8
  153.3 4.2 collective-permute-done.8.refs_2_.refs_5_
  157.4 5.3 collective-permute-done.9.refs_3_.refs_6_
  163.6 37.5 %shard_map.107.chunk_ref = bf16[12288,256]{1,0:T(8,128)(2,1)} custom-call(s32[144]{0:T(256)} %reshape.29.where_ref, s32[48]{0:T(128)} %count_ref.3, s32[1]{0:T(128)} %constant.206.clone.1.turn_ref, bf16[48,3,256,256]{3,2,1,0:T(8,128)(2,1)} %dipole_ref.3, bf16[12288,256]{1,0:T(8,128)(2,1)} %collective-permute-done.7.refs_0_.refs_1_.refs_4_, ...), custom_call_target="tpu_custom_call" | custom-call | flops 1024 | bytes 1024 | tf_op jit(solution)/shard_map/pallas_call | solution.py:95
  201.1 17.7 %shard_map.108 = f32[256,1024]{1,0:T(8,128)} custom-call(bf16[12288,256]{1,0:T(8,128)(2,1)} %shard_map.107.chunk_ref, bf16[12288,1024]{1,0:T(8,128)(2,1)} %upper_ref.9), custom_call_target="tpu_custom_call" | custom-call | flops 1024 | bytes 1024 | tf_op jit(solution)/shard_map/pallas_call | solution.py:126
  221.0 58.1 %collective-permute-done.6.chunk_ref = bf16[12288,256]{1,0:T(8,128)(2,1)} collective-permute-done((bf16[12288,256]{1,0:T(8,128)(2,1)}, bf16[12288,256]{1,0:T(8,128)(2,1)}, u32[]{:S(2)}, u32[]{:S(2)}) %collective-permute-start.6) | collective-permute-done | bytes 6291488 | tf_op jit(solution)/shard_map/ppermute | solution.py:377
  279.1 17.7 %shard_map.109 = f32[256,1024]{1,0:T(8,128)} custom-call(bf16[12288,256]{1,0:T(8,128)(2,1)} %collective-permute-done.6.chunk_ref, bf16[12288,1024]{1,0:T(8,128)(2,1)} %upper_ref.9), custom_call_target="tpu_custom_call" | custom-call | flops 1024 | bytes 1024 | tf_op jit(solution)/shard_map/pallas_call | solution.py:126
  303.4 4.2 collective-permute-start.3
  314.3 58.9 %collective-permute-done.3 = f32[256,1024]{1,0:T(8,128)} collective-permute-done((f32[256,1024]{1,0:T(8,128)S(1)}, f32[256,1024]{1,0:T(8,128)}, u32[]{:S(2)}, u32[]{:S(2)}) %collective-permute-start.3) | collective-permute-done | bytes 1048608 | tf_op jit(solution)/shard_map/ppermute | solution.py:250
  374.9 20.8 %collective-permute-done.4 = f32[256,1024]{1,0:T(8,128)} collective-permute-done((f32[256,1024]{1,0:T(8,128)S(1)}, f32[256,1024]{1,0:T(8,128)}, u32[]{:S(2)}, u32[]{:S(2)}) %collective-permute-start.4) | collective-permute-done | bytes 1048608 | tf_op jit(solution)/shard_map/ppermute | solution.py:250
  400.7 21.5 %collective-permute-done.13 = f32[256,1024]{1,0:T(8,128)} collective-permute-done((f32[256,1024]{1,0:T(8,128)}, f32[256,1024]{1,0:T(8,128)}, u32[]{:S(2)}, u32[]{:S(2)}) %collective-permute-start.13) | collective-permute-done | bytes 1048608 | tf_op jit(solution)/shard_map/ppermute | solution.py:250
  424.5 17.7 %shard_map.110 = f32[256,1024]{1,0:T(8,128)} custom-call(bf16[12288,256]{1,0:T(8,128)(2,1)} %collective-permute-done.15.chunk_ref, bf16[12288,1024]{1,0:T(8,128)(2,1)} %upper_ref.9), custom_call_target="tpu_custom_call" | custom-call | flops 1024 | bytes 1024 | tf_op jit(solution)/shard_map/pallas_call | solution.py:126
  450.6 11.7 %collective-permute-done.17 = f32[128,1024]{1,0:T(8,128)S(1)} collective-permute-done((f32[128,1024]{1,0:T(8,128)S(1)}, f32[128,1024]{1,0:T(8,128)S(1)}, u32[]{:S(2)}, u32[]{:S(2)}) %collective-permute-start.17) | collective-permute-done | bytes 524320 | tf_op jit(solution)/shard_map/ppermute | solution.py:250
  463.8 11.9 %collective-permute-done.19 = f32[128,1024]{1,0:T(8,128)} collective-permute-done((f32[128,1024]{1,0:T(8,128)S(1)}, f32[128,1024]{1,0:T(8,128)}, u32[]{:S(2)}, u32[]{:S(2)}) %collective-permute-start.19) | collective-permute-done | bytes 524320 | tf_op jit(solution)/shard_map/ppermute | solution.py:250
  478.0 3.3 collective-permute-done.14.chunk_ref
  481.3 15.3 %shard_map.111 = f32[128,1024]{1,0:T(8,128)} custom-call(bf16[12288,128]{1,0:T(8,128)(2,1)} %collective-permute-done.14.chunk_ref, bf16[12288,1024]{1,0:T(8,128)(2,1)} %upper_ref.9), custom_call_target="tpu_custom_call" | custom-call | flops 1024 | bytes 1024 | tf_op jit(solution)/shard_map/pallas_call | solution.py:126
  497.6 2.8 collective-permute-start.20
  507.4 3.0 shard_map.112
  514.2 6.4 %collective-permute-done.23 = f32[64,1024]{1,0:T(8,128)S(1)} collective-permute-done((f32[64,1024]{1,0:T(8,128)S(1)}, f32[64,1024]{1,0:T(8,128)S(1)}, u32[]{:S(2)}, u32[]{:S(2)}) %collective-permute-start.23) | collective-permute-done | bytes 262176 | tf_op jit(solution)/shard_map/ppermute | solution.py:250
  523.5 7.3 %fusion = f32[128,1024]{1,0:T(8,128)S(1)} fusion(bf16[7680,128]{1,0:T(8,128)(2,1)} %collective-permute-done.24, bf16[12288,1024]{1,0:T(8,128)(2,1)} %upper_ref.9), kind=kOutput, calls=%fused_computation | convolution fusion | flops 2013265920 | bytes 18219008 | tf_op jit(solution)/shard_map/dot_general | solution.py:138
  530.8 9.6 %collective-permute-done.26 = bf16[3072,128]{1,0:T(8,128)(2,1)} collective-permute-done((bf16[3072,128]{1,0:T(8,128)(2,1)}, bf16[3072,128]{1,0:T(8,128)(2,1)}, u32[]{:S(2)}, u32[]{:S(2)}) %collective-permute-start.26) | collective-permute-done | bytes 786464 | tf_op jit(solution)/shard_map/ppermute | solution.py:377
  540.6 4.1 fusion.2
  544.7 4.7 collective-permute-done.25
  565.2 3.5 collective-permute-done.30.refs_4_
  569.4 3.3 shard_map.113
  (87 shorter events, 76.3 us)
Async XLA Ops:
  7.6 137.8 %collective-permute-start.7 = (bf16[12288,256]{1,0:T(8,128)(2,1)}, bf16[12288,256]{1,0:T(8,128)(2,1)}, u32[]{:S(2)}, u32[]{:S(2)}) collective-permute-start(bf16[12288,256]{1,0:T(8,128)(2,1)} %shard_map.104), channel_id=1, source_target_pairs={{0,2},{2,0},{1,3},{3,1},{4,6},{6,4},{5,7},{7,5},{8,10},{10,8},{9,1... | collective-permute-start | bytes 18874376 | tf_op jit(solution)/shard_map/ppermute | solution.py:377
  12.6 27.3 %collective-permute-start = (bf16[1024,1024]{1,0:T(8,128)(2,1)}, bf16[1024,1024]{1,0:T(8,128)(2,1)S(1)}, u32[]{:S(2)}, u32[]{:S(2)}) collective-permute-start(bf16[1024,1024]{1,0:T(8,128)(2,1)} %get-tuple-element.57), channel_id=1, source_target_pairs={{0,1},{1,4},{4,5},{5,8},{8,9},{9,12},{12,13},{2,3},{3,6},{6,7},{7,... | collective-permute-start | bytes 6291464 | tf_op jit(solution)/shard_map/ppermute | solution.py:219
  16.6 28.0 %collective-permute-start.1 = (bf16[1024,1024]{1,0:T(8,128)(2,1)}, bf16[1024,1024]{1,0:T(8,128)(2,1)}, u32[]{:S(2)}, u32[]{:S(2)}) collective-permute-start(bf16[1024,1024]{1,0:T(8,128)(2,1)} %get-tuple-element.56), channel_id=1, source_target_pairs={{1,0},{4,1},{5,4},{8,5},{9,8},{12,9},{13,12},{3,2},{6,3},{7,6},{10... | collective-permute-start | bytes 6291464 | tf_op jit(solution)/shard_map/ppermute | solution.py:220
  110.9 168.2 %collective-permute-start.6 = (bf16[12288,256]{1,0:T(8,128)(2,1)}, bf16[12288,256]{1,0:T(8,128)(2,1)}, u32[]{:S(2)}, u32[]{:S(2)}) collective-permute-start(bf16[12288,256]{1,0:T(8,128)(2,1)} %get-tuple-element.30), channel_id=1, source_target_pairs={{0,2},{2,0},{1,3},{3,1},{4,6},{6,4},{5,7},{7,5},{8,10},{10,8},{9,1... | collective-permute-start | bytes 18874376 | tf_op jit(solution)/shard_map/ppermute | solution.py:377
  146.6 10.8 %collective-permute-start.8 = (bf16[1024,256]{1,0:T(8,128)(2,1)S(1)}, bf16[1024,256]{1,0:T(8,128)(2,1)S(1)}, u32[]{:S(2)}, u32[]{:S(2)}) collective-permute-start(bf16[1024,256]{1,0:T(8,128)(2,1)S(1)} %get-tuple-element.59), channel_id=1, source_target_pairs={{0,1},{1,4},{4,5},{5,8},{8,9},{9,12},{12,13},{2,3},{3,6},{6,7},{7,... | collective-permute-start | bytes 1572872 | tf_op jit(solution)/shard_map/ppermute | solution.py:219
  151.3 11.4 %collective-permute-start.9 = (bf16[1024,256]{1,0:T(8,128)(2,1)S(1)}, bf16[1024,256]{1,0:T(8,128)(2,1)S(1)}, u32[]{:S(2)}, u32[]{:S(2)}) collective-permute-start(bf16[1024,256]{1,0:T(8,128)(2,1)S(1)} %get-tuple-element.58), channel_id=1, source_target_pairs={{1,0},{4,1},{5,4},{8,5},{9,8},{12,9},{13,12},{3,2},{6,3},{7,6},{10... | collective-permute-start | bytes 1572872 | tf_op jit(solution)/shard_map/ppermute | solution.py:220
  218.8 205.7 %collective-permute-start.15 = (bf16[12288,256]{1,0:T(8,128)(2,1)}, bf16[12288,256]{1,0:T(8,128)(2,1)}, u32[]{:S(2)}, u32[]{:S(2)}) collective-permute-start(bf16[12288,256]{1,0:T(8,128)(2,1)} %get-tuple-element.38), channel_id=1, source_target_pairs={{0,2},{2,0},{1,3},{3,1},{4,6},{6,4},{5,7},{7,5},{8,10},{10,8},{9,1... | collective-permute-start | bytes 18874376 | tf_op jit(solution)/shard_map/ppermute | solution.py:377
  220.8 80.3 %collective-permute-start.2 = (f32[2,256,1024]{2,1,0:T(8,128)S(1)}, f32[2,256,1024]{2,1,0:T(8,128)}, u32[]{:S(2)}, u32[]{:S(2)}) collective-permute-start(f32[2,256,1024]{2,1,0:T(8,128)S(1)} %dynamic-slice_bitcast_fusion), channel_id=1, source_target_pairs={{0,1},{1,0},{2,3},{3,2},{4,5},{5,4},{6,7},{7,6},{8,9},{9,8},{10,11... | collective-permute-start | bytes 6291464 | tf_op jit(solution)/shard_map/ppermute | solution.py:236
  221.0 75.8 %copy-start.2 = (f32[256,1024]{1,0:T(8,128)S(1)}, f32[256,1024]{1,0:T(8,128)}, u32[]{:S(2)}) copy-start(f32[256,1024]{1,0:T(8,128)} %shard_map.108) | copy-start | bytes 3145732
  298.4 13.2 %collective-permute-start.10 = (f32[1,256,1024]{2,1,0:T(8,128)S(1)}, f32[1,256,1024]{2,1,0:T(8,128)S(1)}, u32[]{:S(2)}, u32[]{:S(2)}) collective-permute-start(f32[1,256,1024]{2,1,0:T(8,128)S(1)} %dynamic-slice_bitcast_fusion.1), channel_id=1, source_target_pairs={{0,1},{1,0},{2,3},{3,2},{4,5},{5,4},{6,7},{7,6},{8,9},{9,8},{10,11... | collective-permute-start | bytes 3145736 | tf_op jit(solution)/shard_map/ppermute | solution.py:236
  303.4 69.8 %collective-permute-start.3 = (f32[256,1024]{1,0:T(8,128)S(1)}, f32[256,1024]{1,0:T(8,128)}, u32[]{:S(2)}, u32[]{:S(2)}) collective-permute-start(f32[256,1024]{1,0:T(8,128)S(1)} %get-tuple-element.62), channel_id=1, source_target_pairs={{12,0},{13,1},{0,4},{1,5},{6,10},{7,11},{10,14},{11,15},{28,16},{2... | collective-permute-start | bytes 3145736 | tf_op jit(solution)/shard_map/ppermute | solution.py:250
  307.6 88.1 %collective-permute-start.4 = (f32[256,1024]{1,0:T(8,128)S(1)}, f32[256,1024]{1,0:T(8,128)}, u32[]{:S(2)}, u32[]{:S(2)}) collective-permute-start(f32[256,1024]{1,0:T(8,128)S(1)} %get-tuple-element.60), channel_id=1, source_target_pairs={{8,0},{9,1},{12,4},{13,5},{2,10},{3,11},{6,14},{7,15},{24,16},{25,... | collective-permute-start | bytes 3145736 | tf_op jit(solution)/shard_map/ppermute | solution.py:250
  309.9 88.0 %collective-permute-start.5 = (f32[256,1024]{1,0:T(8,128)S(1)}, f32[256,1024]{1,0:T(8,128)}, u32[]{:S(2)}, u32[]{:S(2)}) collective-permute-start(f32[256,1024]{1,0:T(8,128)S(1)} %get-tuple-element.61), channel_id=1, source_target_pairs={{4,0},{5,1},{8,4},{9,5},{14,10},{15,11},{2,14},{3,15},{20,16},{21,... | collective-permute-start | bytes 3145736 | tf_op jit(solution)/shard_map/ppermute | solution.py:250
  312.7 88.0 %collective-permute-start.11 = (f32[256,1024]{1,0:T(8,128)}, f32[256,1024]{1,0:T(8,128)}, u32[]{:S(2)}, u32[]{:S(2)}) collective-permute-start(f32[256,1024]{1,0:T(8,128)} %fusion.6), channel_id=1, source_target_pairs={{8,12},{9,13},{14,2},{15,3},{24,28},{25,29},{30,18},{31,19}} | collective-permute-start | bytes 3145736 | tf_op jit(solution)/shard_map/ppermute | solution.py:250
  373.2 27.5 %collective-permute-start.12 = (f32[256,1024]{1,0:T(8,128)}, f32[256,1024]{1,0:T(8,128)}, u32[]{:S(2)}, u32[]{:S(2)}) collective-permute-start(f32[256,1024]{1,0:T(8,128)} %fusion.6), channel_id=1, source_target_pairs={{4,12},{5,13},{10,2},{11,3},{20,28},{21,29},{26,18},{27,19}} | collective-permute-start | bytes 3145736 | tf_op jit(solution)/shard_map/ppermute | solution.py:250
  395.7 26.5 %collective-permute-start.13 = (f32[256,1024]{1,0:T(8,128)}, f32[256,1024]{1,0:T(8,128)}, u32[]{:S(2)}, u32[]{:S(2)}) collective-permute-start(f32[256,1024]{1,0:T(8,128)} %fusion.6), channel_id=1, source_target_pairs={{0,12},{1,13},{6,2},{7,3},{16,28},{17,29},{22,18},{23,19}} | collective-permute-start | bytes 3145736 | tf_op jit(solution)/shard_map/ppermute | solution.py:250
  398.0 83.4 %collective-permute-start.14 = (bf16[12288,128]{1,0:T(8,128)(2,1)}, bf16[12288,128]{1,0:T(8,128)(2,1)}, u32[]{:S(2)}, u32[]{:S(2)}) collective-permute-start(bf16[12288,128]{1,0:T(8,128)(2,1)} %get-tuple-element.36), channel_id=1, source_target_pairs={{0,2},{2,0},{1,3},{3,1},{4,6},{6,4},{5,7},{7,5},{8,10},{10,8},{9,1... | collective-permute-start | bytes 9437192 | tf_op jit(solution)/shard_map/ppermute | solution.py:377
  443.2 2.1 collective-permute-start.16
  446.4 15.9 %collective-permute-start.17 = (f32[128,1024]{1,0:T(8,128)S(1)}, f32[128,1024]{1,0:T(8,128)S(1)}, u32[]{:S(2)}, u32[]{:S(2)}) collective-permute-start(f32[128,1024]{1,0:T(8,128)S(1)} %fusion.9), channel_id=1, source_target_pairs={{4,8},{5,9},{2,6},{3,7},{20,24},{21,25},{18,22},{19,23}} | collective-permute-start | bytes 1572872 | tf_op jit(solution)/shard_map/ppermute | solution.py:250
  447.7 16.1 %collective-permute-start.18 = (f32[128,1024]{1,0:T(8,128)S(1)}, f32[128,1024]{1,0:T(8,128)}, u32[]{:S(2)}, u32[]{:S(2)}) collective-permute-start(f32[128,1024]{1,0:T(8,128)S(1)} %fusion.9), channel_id=1, source_target_pairs={{0,8},{1,9},{14,6},{15,7},{16,24},{17,25},{30,22},{31,23}} | collective-permute-start | bytes 1572872 | tf_op jit(solution)/shard_map/ppermute | solution.py:250
  449.0 26.7 %collective-permute-start.19 = (f32[128,1024]{1,0:T(8,128)S(1)}, f32[128,1024]{1,0:T(8,128)}, u32[]{:S(2)}, u32[]{:S(2)}) collective-permute-start(f32[128,1024]{1,0:T(8,128)S(1)} %fusion.9), channel_id=1, source_target_pairs={{12,8},{13,9},{10,6},{11,7},{28,24},{29,25},{26,22},{27,23}} | collective-permute-start | bytes 1572872 | tf_op jit(solution)/shard_map/ppermute | solution.py:250
  450.5 73.0 %collective-permute-start.24 = (bf16[7680,128]{1,0:T(8,128)(2,1)}, bf16[7680,128]{1,0:T(8,128)(2,1)}, u32[]{:S(2)}, u32[]{:S(2)}) collective-permute-start(bf16[7680,128]{1,0:T(8,128)(2,1)} %get-tuple-element.45), channel_id=1, source_target_pairs={{0,2},{2,0},{1,3},{3,1},{4,6},{6,4},{5,7},{7,5},{8,10},{10,8},{9,1... | collective-permute-start | bytes 5898248 | tf_op jit(solution)/shard_map/ppermute | solution.py:377
  497.6 3.9 collective-permute-start.20
  502.5 9.5 %collective-permute-start.21 = (f32[64,1024]{1,0:T(8,128)S(1)}, f32[64,1024]{1,0:T(8,128)S(1)}, u32[]{:S(2)}, u32[]{:S(2)}) collective-permute-start(f32[64,1024]{1,0:T(8,128)S(1)} %fusion.10), channel_id=1, source_target_pairs={{4,8},{5,9},{2,6},{3,7},{20,24},{21,25},{18,22},{19,23}} | collective-permute-start | bytes 786440 | tf_op jit(solution)/shard_map/ppermute | solution.py:250
  503.8 10.4 %collective-permute-start.22 = (f32[64,1024]{1,0:T(8,128)S(1)}, f32[64,1024]{1,0:T(8,128)S(1)}, u32[]{:S(2)}, u32[]{:S(2)}) collective-permute-start(f32[64,1024]{1,0:T(8,128)S(1)} %fusion.10), channel_id=1, source_target_pairs={{0,8},{1,9},{14,6},{15,7},{16,24},{17,25},{30,22},{31,23}} | collective-permute-start | bytes 786440 | tf_op jit(solution)/shard_map/ppermute | solution.py:250
  505.1 15.5 %collective-permute-start.23 = (f32[64,1024]{1,0:T(8,128)S(1)}, f32[64,1024]{1,0:T(8,128)S(1)}, u32[]{:S(2)}, u32[]{:S(2)}) collective-permute-start(f32[64,1024]{1,0:T(8,128)S(1)} %fusion.10), channel_id=1, source_target_pairs={{12,8},{13,9},{10,6},{11,7},{28,24},{29,25},{26,22},{27,23}} | collective-permute-start | bytes 786440 | tf_op jit(solution)/shard_map/ppermute | solution.py:250
  506.4 33.9 %collective-permute-start.26 = (bf16[3072,128]{1,0:T(8,128)(2,1)}, bf16[3072,128]{1,0:T(8,128)(2,1)}, u32[]{:S(2)}, u32[]{:S(2)}) collective-permute-start(bf16[3072,128]{1,0:T(8,128)(2,1)} %get-tuple-element.48), channel_id=1, source_target_pairs={{0,2},{2,0},{1,3},{3,1},{4,6},{6,4},{5,7},{7,5},{8,10},{10,8},{9,1... | collective-permute-start | bytes 2359304 | tf_op jit(solution)/shard_map/ppermute | solution.py:377
  540.3 9.1 %collective-permute-start.25 = (bf16[1536,128]{1,0:T(8,128)(2,1)S(1)}, bf16[1536,128]{1,0:T(8,128)(2,1)S(1)}, u32[]{:S(2)}, u32[]{:S(2)}) collective-permute-start(bf16[1536,128]{1,0:T(8,128)(2,1)S(1)} %copy-done.9), channel_id=1, source_target_pairs={{0,2},{2,0},{1,3},{3,1},{4,6},{6,4},{5,7},{7,5},{8,10},{10,8},{9,1... | collective-permute-start | bytes 1179656 | tf_op jit(solution)/shard_map/ppermute | solution.py:377
  552.0 3.7 collective-permute-start.27
  556.4 6.6 %collective-permute-start.28 = (bf16[64,1024]{1,0:T(8,128)(2,1)S(1)}, bf16[64,1024]{1,0:T(8,128)(2,1)S(1)}, u32[]{:S(2)}, u32[]{:S(2)}) collective-permute-start(bf16[64,1024]{1,0:T(8,128)(2,1)S(1)} %get-tuple-element.64), channel_id=1, source_target_pairs={{4,8},{5,9},{2,6},{3,7},{20,24},{21,25},{18,22},{19,23}} | collective-permute-start | bytes 393224 | tf_op jit(solution)/shard_map/ppermute | solution.py:250
  557.7 7.5 %collective-permute-start.29 = (bf16[64,1024]{1,0:T(8,128)(2,1)S(1)}, bf16[64,1024]{1,0:T(8,128)(2,1)S(1)}, u32[]{:S(2)}, u32[]{:S(2)}) collective-permute-start(bf16[64,1024]{1,0:T(8,128)(2,1)S(1)} %get-tuple-element.64), channel_id=1, source_target_pairs={{0,8},{1,9},{14,6},{15,7},{16,24},{17,25},{30,22},{31,23}} | collective-permute-start | bytes 393224 | tf_op jit(solution)/shard_map/ppermute | solution.py:250
  559.0 9.7 %collective-permute-start.30 = (bf16[64,1024]{1,0:T(8,128)(2,1)S(1)}, bf16[64,1024]{1,0:T(8,128)(2,1)S(1)}, u32[]{:S(2)}, u32[]{:S(2)}) collective-permute-start(bf16[64,1024]{1,0:T(8,128)(2,1)S(1)} %get-tuple-element.64), channel_id=1, source_target_pairs={{12,8},{13,9},{10,6},{11,7},{28,24},{29,25},{26,22},{27,23}} | collective-permute-start | bytes 393224 | tf_op jit(solution)/shard_map/ppermute | solution.py:250
  (9 other events, 54.9 us)

commit v3 on v2

--- a/solution.py
+++ b/solution.py
@@ -195,12 +195,12 @@
 
 
 def columns(array, at, width):
-    step = array.shape[0] // 6
+    step = array.shape[0] // 2
     return pl.pallas_call(
         copy_kernel,
         grid_spec=pltpu.PrefetchScalarGridSpec(
             num_scalar_prefetch=1,
-            grid=(6,),
+            grid=(2,),
             in_specs=[pl.BlockSpec((step, width), lambda i, at_ref: (i, at_ref[0]))],
             out_specs=pl.BlockSpec((step, width), lambda i, at_ref: (i, 0)),
         ),
@@ -225,21 +225,26 @@
     return (row * lax.axis_size("win") + win) * lax.axis_size("rep") + core
 
 
-def to_chips(partial, groups, chip, wire=jnp.float32):
-    rows, wins, reps = (lax.axis_size(axis) for axis in AXES)
-    row, win, rep = (lax.axis_index(axis) for axis in AXES)
+def of_chip(partial, groups):
+    reps, rep = lax.axis_size("rep"), lax.axis_index("rep")
     split = partial.reshape(groups, reps, -1, partial.shape[1])
     of_core = lambda core: lax.dynamic_index_in_dim(split, core, 1, keepdims=False)
     mine = of_core(rep)
     for turn in range(1, reps):
         pairs = [(i, (i + turn) % reps) for i in range(reps)]
         mine = mine + lax.ppermute(of_core((rep + turn) % reps), "rep", pairs)
+    return mine
+
+
+def to_chips(partial, groups, chip):
+    rows, wins, reps = (lax.axis_size(axis) for axis in AXES)
+    row, win, _ = (lax.axis_index(axis) for axis in AXES)
+    mine = of_chip(partial, groups)
     first = functools.reduce(lambda at, w: jnp.where(win == w, chip(w), at), range(1, wins), chip(0))
     terms = []
-    sent = mine.astype(wire)
     for turn in [*range(rows - 1, 0, -1), 0]:
         at = (row - turn - first) % rows
-        piece = lax.dynamic_index_in_dim(sent if turn else mine, jnp.minimum(at, groups - 1), 0, keepdims=False)
+        piece = lax.dynamic_index_in_dim(mine, jnp.minimum(at, groups - 1), 0, keepdims=False)
         if turn:
             pairs = [
                 (place((chip(w) + g + turn) % rows, w, core), place(chip(w) + g, w, core))
@@ -251,6 +256,27 @@
         else:
             terms.append(jnp.where(at < groups, piece, 0.0))
     return terms
+
+
+def to_chip(partial, chip):
+    rows, wins, reps = (lax.axis_size(axis) for axis in AXES)
+    row, win, _ = (lax.axis_index(axis) for axis in AXES)
+    mine = of_chip(partial, 1)[0]
+    sent = mine.astype(jnp.bfloat16)
+
+    def sources(w):
+        at = chip(w)
+        rank = lambda other: (-abs(other - at), (other > at) != (2 * at < rows))
+        return sorted((other for other in range(rows) if other != at), key=rank)
+
+    terms = []
+    for index in range(rows - 1):
+        pairs = [
+            (place(sources(w)[index], w, core), place(chip(w), w, core)) for w in range(wins) for core in range(reps)
+        ]
+        terms.append(lax.ppermute(sent, AXES, pairs))
+    owner = functools.reduce(lambda at, w: jnp.where(win == w, chip(w), at), range(1, wins), chip(0))
+    return [*terms, jnp.where(row == owner, mine, 0.0)]
 
 
 def shards(
@@ -296,7 +322,7 @@
             at = [start + core * share for core in range(reps)]
             plan.append(("whole", g, tuple((i,) for i in at), 0, rows_here, (0, LANES)))
             plan.append(("whole", g, (tuple(i + LANES for i in at),), 0, rows_here, (LANES, tail)))
-            cuts = [0, rows_here * 5 // 8, rows_here * 7 // 8, rows_here]
+            cuts = [0, rows_here * 13 // 16, rows_here]
             for top, bottom in zip(cuts, cuts[1:]):
                 plan.append(("cut", g, (tuple(i + LANES + tail for i in at),), top, bottom, None))
             continue
@@ -334,7 +360,7 @@
             if bottom < rows_here:
                 waiting.append(part)
             else:
-                late.extend(to_chips(part, 1, chip, jnp.bfloat16))
+                late.extend(to_chip(part, chip))
             return part
         if kind == "raw":
             ends = halo(piece[-width:], piece[:width], owners)

time: 577 us -> 572 us (level)
  waiting for transfers between devices: 261 us -> 251 us
    ppermute x15 -> x12, waiting for transfers between devices: 145 us -> 136 us  [to_chips(): terms.append(lax.ppermute(piece, AXES, pairs))]
    ppermute x5 -> x8, starting transfers between devices: 8.66 us -> 16.7 us  [the longest x5 12.8 us: of_chip(): mine = mine + lax.ppermute(of_core((rep + turn) % reps), 'rep', pairs)]
    ppermute x5 -> x8, waiting for transfers between devices: 3.87 us -> 11 us  [the longest x3 7.14 us: to_chip(): terms.append(lax.ppermute(sent, AXES, pairs))]
    ppermute x7 -> x6, waiting for transfers between devices: 77.6 us -> 72.6 us  [shards(): lax.ppermute(array, 'win', [(i, (i + step) % wins) for i in range(wins)])]
    ppermute x15 -> x12, starting transfers between devices: 25.5 us -> 21.7 us  [to_chips(): terms.append(lax.ppermute(piece, AXES, pairs))]
    dot_general x3 -> x2, matrix products: 13.8 us -> 12.4 us  [part_product(): lax.dot_general(chunk, eig_upper[first:first + chunk.shape[0]], (((0,), (...]
  transfers between devices with their start and end apart: 31 -> 30, of which waited for: 24 -> 22; matrix products, arithmetic and copies ran while one was open for 6% -> 6% of each run, Pallas kernels for 36% -> 38%
where the time goes in v3:
time: 572 us; the launch traced here: 569 us
  waiting for transfers between devices  251 us (44%)
  Pallas kernels  222 us (39%)
  starting transfers between devices  54.7 us (10%)
  other arithmetic  15.2 us (3%)
  local copies, waits for them, and re-layouts  12.5 us (2%)
  matrix products  12.4 us (2%)
    ppermute x12, waiting for transfers between devices, to_chips(): terms.append(lax.ppermute(piece, AXES, pairs))  136 us
    pallas_call x2, Pallas kernels, image(): pl.pallas_call(functools.partial(image_kernel, slots, pieces), grid_spec=...  109 us
    pallas_call x5, Pallas kernels, product(): pl.pallas_call(product_kernel, grid=(depth // step,), in_specs=[pl.BlockS...  101 us
    ppermute x6, waiting for transfers between devices, shards(): lax.ppermute(array, 'win', [(i, (i + step) % wins) for i in range(wins)])  72.6 us
    ppermute x12, starting transfers between devices, to_chips(): terms.append(lax.ppermute(piece, AXES, pairs))  21.7 us
    ppermute x2, waiting for transfers between devices, halo(): low = lax.ppermute(last, axes, up)  21.5 us
    ppermute x5, starting transfers between devices, of_chip(): mine = mine + lax.ppermute(of_core((rep + turn) % reps), 'rep', pairs)  12.8 us
    dot_general x2, matrix products, part_product(): lax.dot_general(chunk, eig_upper[first:first + chunk.shape[0]], (((0,), (...  12.4 us
  transfers between devices with their start and end apart: 30, of which 22 were waited for; matrix products, arithmetic and copies ran while one was open for 6% of the time, Pallas kernels for 38%

profile of v3, /device:TPU:11, one launch (start us, length us, event | category | flops | bytes accessed | tf_op | source)
XLA Modules:
  0.0 568.5 jit_solution(14309886986768804787)
XLA Ops:
  0.7 4.8 shard_map.104
  5.7 4.7 fusion.9
  10.4 4.0 collective-permute-start
  17.2 20.6 %collective-permute-done.refs_2_.refs_5_ = bf16[1024,1024]{1,0:T(8,128)(2,1)S(1)} collective-permute-done((bf16[1024,1024]{1,0:T(8,128)(2,1)}, bf16[1024,1024]{1,0:T(8,128)(2,1)S(1)}, u32[]{:S(2)}, u32[]{:S(2)}) %collective-permute-start) | collective-permute-done | bytes 2097184 | tf_op jit(solution)/shard_map/ppermute | solution.py:219
  37.7 4.7 collective-permute-done.1.refs_3_.refs_6_
  42.4 69.1 %shard_map.105 = (bf16[12288,1024]{1,0:T(8,128)(2,1)}, bf16[12288,256]{1,0:T(8,128)(2,1)}, bf16[12288,256]{1,0:T(8,128)(2,1)}, bf16[12288,128]{1,0:T(8,128)(2,1)...) custom-call(s32[144]{0:T(256)} %reshape.30.where_ref, s32[48]{0:T(128)} %count_ref.3, s32[1]{0:T(128)} %bitcast.4.turn_ref, ...), custom_call_target="tpu_custom_call" | custom-call | flops 1024 | bytes 1024 | tf_op jit(solution)/shard_map/pallas_call | solution.py:95
  112.8 33.1 %shard_map.106 = f32[1024,1024]{1,0:T(8,128)} custom-call(bf16[12288,1024]{1,0:T(8,128)(2,1)} %get-tuple-element.25.chunk_ref, bf16[12288,1024]{1,0:T(8,128)(2,1)} %upper_ref.9), custom_call_target="tpu_custom_call" | custom-call | flops 1024 | bytes 1024 | tf_op jit(solution)/shard_map/pallas_call | solution.py:126
  149.2 5.1 collective-permute-start.9
  155.3 4.8 collective-permute-done.9.refs_3_.refs_6_
  160.9 40.1 %shard_map.107.chunk_ref = bf16[12288,256]{1,0:T(8,128)(2,1)} custom-call(s32[144]{0:T(256)} %reshape.30.where_ref, s32[48]{0:T(128)} %count_ref.3, s32[1]{0:T(128)} %constant.188.clone.1.turn_ref, bf16[48,3,256,256]{3,2,1,0:T(8,128)(2,1)} %dipole_ref.3, bf16[12288,256]{1,0:T(8,128)(2,1)} %collective-permute-done.7.refs_0_.refs_1_.refs_4_, ...), custom_call_target="tpu_custom_call" | custom-call | flops 1024 | bytes 1024 | tf_op jit(solution)/shard_map/pallas_call | solution.py:95
  201.0 17.7 %shard_map.108 = f32[256,1024]{1,0:T(8,128)} custom-call(bf16[12288,256]{1,0:T(8,128)(2,1)} %shard_map.107.chunk_ref, bf16[12288,1024]{1,0:T(8,128)(2,1)} %upper_ref.9), custom_call_target="tpu_custom_call" | custom-call | flops 1024 | bytes 1024 | tf_op jit(solution)/shard_map/pallas_call | solution.py:126
  220.7 5.1 collective-permute-start.2
  225.9 51.1 %collective-permute-done.6.chunk_ref = bf16[12288,256]{1,0:T(8,128)(2,1)} collective-permute-done((bf16[12288,256]{1,0:T(8,128)(2,1)}, bf16[12288,256]{1,0:T(8,128)(2,1)}, u32[]{:S(2)}, u32[]{:S(2)}) %collective-permute-start.6) | collective-permute-done | bytes 6291488 | tf_op jit(solution)/shard_map/ppermute | solution.py:403
  277.0 17.7 %shard_map.109 = f32[256,1024]{1,0:T(8,128)} custom-call(bf16[12288,256]{1,0:T(8,128)(2,1)} %collective-permute-done.6.chunk_ref, bf16[12288,1024]{1,0:T(8,128)(2,1)} %upper_ref.9), custom_call_target="tpu_custom_call" | custom-call | flops 1024 | bytes 1024 | tf_op jit(solution)/shard_map/pallas_call | solution.py:126
  301.3 4.2 collective-permute-start.3
  312.2 58.9 %collective-permute-done.3 = f32[256,1024]{1,0:T(8,128)} collective-permute-done((f32[256,1024]{1,0:T(8,128)S(1)}, f32[256,1024]{1,0:T(8,128)}, u32[]{:S(2)}, u32[]{:S(2)}) %collective-permute-start.3) | collective-permute-done | bytes 1048608 | tf_op jit(solution)/shard_map/ppermute | solution.py:255
  372.7 20.8 %collective-permute-done.4 = f32[256,1024]{1,0:T(8,128)} collective-permute-done((f32[256,1024]{1,0:T(8,128)S(1)}, f32[256,1024]{1,0:T(8,128)}, u32[]{:S(2)}, u32[]{:S(2)}) %collective-permute-start.4) | collective-permute-done | bytes 1048608 | tf_op jit(solution)/shard_map/ppermute | solution.py:255
  398.6 21.4 %collective-permute-done.13 = f32[256,1024]{1,0:T(8,128)} collective-permute-done((f32[256,1024]{1,0:T(8,128)}, f32[256,1024]{1,0:T(8,128)}, u32[]{:S(2)}, u32[]{:S(2)}) %collective-permute-start.13) | collective-permute-done | bytes 1048608 | tf_op jit(solution)/shard_map/ppermute | solution.py:255
  422.3 17.7 %shard_map.110 = f32[256,1024]{1,0:T(8,128)} custom-call(bf16[12288,256]{1,0:T(8,128)(2,1)} %collective-permute-done.15.chunk_ref, bf16[12288,1024]{1,0:T(8,128)(2,1)} %upper_ref.9), custom_call_target="tpu_custom_call" | custom-call | flops 1024 | bytes 1024 | tf_op jit(solution)/shard_map/pallas_call | solution.py:126
  448.4 11.8 %collective-permute-done.17 = f32[128,1024]{1,0:T(8,128)S(1)} collective-permute-done((f32[128,1024]{1,0:T(8,128)S(1)}, f32[128,1024]{1,0:T(8,128)S(1)}, u32[]{:S(2)}, u32[]{:S(2)}) %collective-permute-start.17) | collective-permute-done | bytes 524320 | tf_op jit(solution)/shard_map/ppermute | solution.py:255
  461.7 11.9 %collective-permute-done.19 = f32[128,1024]{1,0:T(8,128)} collective-permute-done((f32[128,1024]{1,0:T(8,128)S(1)}, f32[128,1024]{1,0:T(8,128)}, u32[]{:S(2)}, u32[]{:S(2)}) %collective-permute-start.19) | collective-permute-done | bytes 524320 | tf_op jit(solution)/shard_map/ppermute | solution.py:255
  475.9 3.3 collective-permute-done.14.chunk_ref
  479.2 15.3 %shard_map.111 = f32[128,1024]{1,0:T(8,128)} custom-call(bf16[12288,128]{1,0:T(8,128)(2,1)} %collective-permute-done.14.chunk_ref, bf16[12288,1024]{1,0:T(8,128)(2,1)} %upper_ref.9), custom_call_target="tpu_custom_call" | custom-call | flops 1024 | bytes 1024 | tf_op jit(solution)/shard_map/pallas_call | solution.py:126
  505.3 3.0 shard_map.112
  512.0 6.4 %collective-permute-done.23 = f32[64,1024]{1,0:T(8,128)S(1)} collective-permute-done((f32[64,1024]{1,0:T(8,128)S(1)}, f32[64,1024]{1,0:T(8,128)S(1)}, u32[]{:S(2)}, u32[]{:S(2)}) %collective-permute-start.23) | collective-permute-done | bytes 262176 | tf_op jit(solution)/shard_map/ppermute | solution.py:255
  519.3 14.6 %collective-permute-done.25 = bf16[9984,128]{1,0:T(8,128)(2,1)} collective-permute-done((bf16[9984,128]{1,0:T(8,128)(2,1)}, bf16[9984,128]{1,0:T(8,128)(2,1)}, u32[]{:S(2)}, u32[]{:S(2)}) %collective-permute-start.25) | collective-permute-done | bytes 2555936 | tf_op jit(solution)/shard_map/ppermute | solution.py:403
  534.0 9.1 %fusion = f32[128,1024]{1,0:T(8,128)S(1)} fusion(bf16[9984,128]{1,0:T(8,128)(2,1)} %collective-permute-done.25, bf16[12288,1024]{1,0:T(8,128)(2,1)} %upper_ref.9), kind=kOutput, calls=%fused_computation | convolution fusion | flops 2617245696 | bytes 23527424 | tf_op jit(solution)/shard_map/dot_general | solution.py:138
  543.1 3.5 collective-permute-done.24
  546.6 3.3 fusion.2
  557.4 3.6 collective-permute-done.27.refs_2_
  561.1 3.5 collective-permute-done.28.refs_3_
  565.3 3.3 shard_map.113
  (81 shorter events, 69.4 us)
Async XLA Ops:
  5.4 11.0 %copy-start.8 = (s32[48,3]{0,1:T(4,128)S(1)}, s32[48,3]{0,1:T(4,128)}, u32[]{:S(2)}) copy-start(s32[48,3]{0,1:T(4,128)} %param.12) | copy-start | bytes 1732
  5.4 140.5 %collective-permute-start.7 = (bf16[12288,256]{1,0:T(8,128)(2,1)}, bf16[12288,256]{1,0:T(8,128)(2,1)}, u32[]{:S(2)}, u32[]{:S(2)}) collective-permute-start(bf16[12288,256]{1,0:T(8,128)(2,1)} %shard_map.104), channel_id=1, source_target_pairs={{0,2},{2,0},{1,3},{3,1},{4,6},{6,4},{5,7},{7,5},{8,10},{10,8},{9,1... | collective-permute-start | bytes 18874376 | tf_op jit(solution)/shard_map/ppermute | solution.py:403
  10.4 27.3 %collective-permute-start = (bf16[1024,1024]{1,0:T(8,128)(2,1)}, bf16[1024,1024]{1,0:T(8,128)(2,1)S(1)}, u32[]{:S(2)}, u32[]{:S(2)}) collective-permute-start(bf16[1024,1024]{1,0:T(8,128)(2,1)} %get-tuple-element.49), channel_id=1, source_target_pairs={{0,1},{1,4},{4,5},{5,8},{8,9},{9,12},{12,13},{2,3},{3,6},{6,7},{7,... | collective-permute-start | bytes 6291464 | tf_op jit(solution)/shard_map/ppermute | solution.py:219
  14.5 28.0 %collective-permute-start.1 = (bf16[1024,1024]{1,0:T(8,128)(2,1)}, bf16[1024,1024]{1,0:T(8,128)(2,1)}, u32[]{:S(2)}, u32[]{:S(2)}) collective-permute-start(bf16[1024,1024]{1,0:T(8,128)(2,1)} %get-tuple-element.48), channel_id=1, source_target_pairs={{1,0},{4,1},{5,4},{8,5},{9,8},{12,9},{13,12},{3,2},{6,3},{7,6},{10... | collective-permute-start | bytes 6291464 | tf_op jit(solution)/shard_map/ppermute | solution.py:220
  111.5 165.5 %collective-permute-start.6 = (bf16[12288,256]{1,0:T(8,128)(2,1)}, bf16[12288,256]{1,0:T(8,128)(2,1)}, u32[]{:S(2)}, u32[]{:S(2)}) collective-permute-start(bf16[12288,256]{1,0:T(8,128)(2,1)} %get-tuple-element.26), channel_id=1, source_target_pairs={{0,2},{2,0},{1,3},{3,1},{4,6},{6,4},{5,7},{7,5},{8,10},{10,8},{9,1... | collective-permute-start | bytes 18874376 | tf_op jit(solution)/shard_map/ppermute | solution.py:403
  147.2 8.1 %collective-permute-start.8 = (bf16[1024,256]{1,0:T(8,128)(2,1)S(1)}, bf16[1024,256]{1,0:T(8,128)(2,1)S(1)}, u32[]{:S(2)}, u32[]{:S(2)}) collective-permute-start(bf16[1024,256]{1,0:T(8,128)(2,1)S(1)} %get-tuple-element.51), channel_id=1, source_target_pairs={{0,1},{1,4},{4,5},{5,8},{8,9},{9,12},{12,13},{2,3},{3,6},{6,7},{7,... | collective-permute-start | bytes 1572872 | tf_op jit(solution)/shard_map/ppermute | solution.py:219
  149.2 10.9 %collective-permute-start.9 = (bf16[1024,256]{1,0:T(8,128)(2,1)S(1)}, bf16[1024,256]{1,0:T(8,128)(2,1)S(1)}, u32[]{:S(2)}, u32[]{:S(2)}) collective-permute-start(bf16[1024,256]{1,0:T(8,128)(2,1)S(1)} %get-tuple-element.50), channel_id=1, source_target_pairs={{1,0},{4,1},{5,4},{8,5},{9,8},{12,9},{13,12},{3,2},{6,3},{7,6},{10... | collective-permute-start | bytes 1572872 | tf_op jit(solution)/shard_map/ppermute | solution.py:220
  218.6 203.7 %collective-permute-start.15 = (bf16[12288,256]{1,0:T(8,128)(2,1)}, bf16[12288,256]{1,0:T(8,128)(2,1)}, u32[]{:S(2)}, u32[]{:S(2)}) collective-permute-start(bf16[12288,256]{1,0:T(8,128)(2,1)} %get-tuple-element.34), channel_id=1, source_target_pairs={{0,2},{2,0},{1,3},{3,1},{4,6},{6,4},{5,7},{7,5},{8,10},{10,8},{9,1... | collective-permute-start | bytes 18874376 | tf_op jit(solution)/shard_map/ppermute | solution.py:403
  220.7 78.3 %collective-permute-start.2 = (f32[2,256,1024]{2,1,0:T(8,128)S(1)}, f32[2,256,1024]{2,1,0:T(8,128)}, u32[]{:S(2)}, u32[]{:S(2)}) collective-permute-start(f32[2,256,1024]{2,1,0:T(8,128)S(1)} %dynamic-slice_bitcast_fusion), channel_id=1, source_target_pairs={{0,1},{1,0},{2,3},{3,2},{4,5},{5,4},{6,7},{7,6},{8,9},{9,8},{10,11... | collective-permute-start | bytes 6291464 | tf_op jit(solution)/shard_map/ppermute | solution.py:235
  225.9 68.7 %copy-start.2 = (f32[256,1024]{1,0:T(8,128)S(1)}, f32[256,1024]{1,0:T(8,128)}, u32[]{:S(2)}) copy-start(f32[256,1024]{1,0:T(8,128)} %shard_map.108) | copy-start | bytes 3145732
  296.3 13.2 %collective-permute-start.10 = (f32[1,256,1024]{2,1,0:T(8,128)S(1)}, f32[1,256,1024]{2,1,0:T(8,128)S(1)}, u32[]{:S(2)}, u32[]{:S(2)}) collective-permute-start(f32[1,256,1024]{2,1,0:T(8,128)S(1)} %dynamic-slice_bitcast_fusion.1), channel_id=1, source_target_pairs={{0,1},{1,0},{2,3},{3,2},{4,5},{5,4},{6,7},{7,6},{8,9},{9,8},{10,11... | collective-permute-start | bytes 3145736 | tf_op jit(solution)/shard_map/ppermute | solution.py:235
  301.3 69.8 %collective-permute-start.3 = (f32[256,1024]{1,0:T(8,128)S(1)}, f32[256,1024]{1,0:T(8,128)}, u32[]{:S(2)}, u32[]{:S(2)}) collective-permute-start(f32[256,1024]{1,0:T(8,128)S(1)} %get-tuple-element.54), channel_id=1, source_target_pairs={{12,0},{13,1},{0,4},{1,5},{6,10},{7,11},{10,14},{11,15},{28,16},{2... | collective-permute-start | bytes 3145736 | tf_op jit(solution)/shard_map/ppermute | solution.py:255
  305.4 88.1 %collective-permute-start.4 = (f32[256,1024]{1,0:T(8,128)S(1)}, f32[256,1024]{1,0:T(8,128)}, u32[]{:S(2)}, u32[]{:S(2)}) collective-permute-start(f32[256,1024]{1,0:T(8,128)S(1)} %get-tuple-element.52), channel_id=1, source_target_pairs={{8,0},{9,1},{12,4},{13,5},{2,10},{3,11},{6,14},{7,15},{24,16},{25,... | collective-permute-start | bytes 3145736 | tf_op jit(solution)/shard_map/ppermute | solution.py:255
  307.8 88.0 %collective-permute-start.5 = (f32[256,1024]{1,0:T(8,128)S(1)}, f32[256,1024]{1,0:T(8,128)}, u32[]{:S(2)}, u32[]{:S(2)}) collective-permute-start(f32[256,1024]{1,0:T(8,128)S(1)} %get-tuple-element.53), channel_id=1, source_target_pairs={{4,0},{5,1},{8,4},{9,5},{14,10},{15,11},{2,14},{3,15},{20,16},{21,... | collective-permute-start | bytes 3145736 | tf_op jit(solution)/shard_map/ppermute | solution.py:255
  310.5 88.0 %collective-permute-start.11 = (f32[256,1024]{1,0:T(8,128)}, f32[256,1024]{1,0:T(8,128)}, u32[]{:S(2)}, u32[]{:S(2)}) collective-permute-start(f32[256,1024]{1,0:T(8,128)} %fusion.4), channel_id=1, source_target_pairs={{8,12},{9,13},{14,2},{15,3},{24,28},{25,29},{30,18},{31,19}} | collective-permute-start | bytes 3145736 | tf_op jit(solution)/shard_map/ppermute | solution.py:255
  371.1 27.5 %collective-permute-start.12 = (f32[256,1024]{1,0:T(8,128)}, f32[256,1024]{1,0:T(8,128)}, u32[]{:S(2)}, u32[]{:S(2)}) collective-permute-start(f32[256,1024]{1,0:T(8,128)} %fusion.4), channel_id=1, source_target_pairs={{4,12},{5,13},{10,2},{11,3},{20,28},{21,29},{26,18},{27,19}} | collective-permute-start | bytes 3145736 | tf_op jit(solution)/shard_map/ppermute | solution.py:255
  393.5 26.5 %collective-permute-start.13 = (f32[256,1024]{1,0:T(8,128)}, f32[256,1024]{1,0:T(8,128)}, u32[]{:S(2)}, u32[]{:S(2)}) collective-permute-start(f32[256,1024]{1,0:T(8,128)} %fusion.4), channel_id=1, source_target_pairs={{0,12},{1,13},{6,2},{7,3},{16,28},{17,29},{22,18},{23,19}} | collective-permute-start | bytes 3145736 | tf_op jit(solution)/shard_map/ppermute | solution.py:255
  395.8 83.4 %collective-permute-start.14 = (bf16[12288,128]{1,0:T(8,128)(2,1)}, bf16[12288,128]{1,0:T(8,128)(2,1)}, u32[]{:S(2)}, u32[]{:S(2)}) collective-permute-start(bf16[12288,128]{1,0:T(8,128)(2,1)} %get-tuple-element.32), channel_id=1, source_target_pairs={{0,2},{2,0},{1,3},{3,1},{4,6},{6,4},{5,7},{7,5},{8,10},{10,8},{9,1... | collective-permute-start | bytes 9437192 | tf_op jit(solution)/shard_map/ppermute | solution.py:403
  441.1 2.1 collective-permute-start.16
  441.6 92.3 %collective-permute-start.25 = (bf16[9984,128]{1,0:T(8,128)(2,1)}, bf16[9984,128]{1,0:T(8,128)(2,1)}, u32[]{:S(2)}, u32[]{:S(2)}) collective-permute-start(bf16[9984,128]{1,0:T(8,128)(2,1)} %get-tuple-element.42), channel_id=1, source_target_pairs={{0,2},{2,0},{1,3},{3,1},{4,6},{6,4},{5,7},{7,5},{8,10},{10,8},{9,1... | collective-permute-start | bytes 7667720 | tf_op jit(solution)/shard_map/ppermute | solution.py:403
  444.3 15.9 %collective-permute-start.17 = (f32[128,1024]{1,0:T(8,128)S(1)}, f32[128,1024]{1,0:T(8,128)S(1)}, u32[]{:S(2)}, u32[]{:S(2)}) collective-permute-start(f32[128,1024]{1,0:T(8,128)S(1)} %fusion.7), channel_id=1, source_target_pairs={{4,8},{5,9},{2,6},{3,7},{20,24},{21,25},{18,22},{19,23}} | collective-permute-start | bytes 1572872 | tf_op jit(solution)/shard_map/ppermute | solution.py:255
  445.6 16.1 %collective-permute-start.18 = (f32[128,1024]{1,0:T(8,128)S(1)}, f32[128,1024]{1,0:T(8,128)}, u32[]{:S(2)}, u32[]{:S(2)}) collective-permute-start(f32[128,1024]{1,0:T(8,128)S(1)} %fusion.7), channel_id=1, source_target_pairs={{0,8},{1,9},{14,6},{15,7},{16,24},{17,25},{30,22},{31,23}} | collective-permute-start | bytes 1572872 | tf_op jit(solution)/shard_map/ppermute | solution.py:255
  446.9 26.7 %collective-permute-start.19 = (f32[128,1024]{1,0:T(8,128)S(1)}, f32[128,1024]{1,0:T(8,128)}, u32[]{:S(2)}, u32[]{:S(2)}) collective-permute-start(f32[128,1024]{1,0:T(8,128)S(1)} %fusion.7), channel_id=1, source_target_pairs={{12,8},{13,9},{10,6},{11,7},{28,24},{29,25},{26,22},{27,23}} | collective-permute-start | bytes 1572872 | tf_op jit(solution)/shard_map/ppermute | solution.py:255
  495.4 3.9 collective-permute-start.20
  500.4 9.5 %collective-permute-start.21 = (f32[64,1024]{1,0:T(8,128)S(1)}, f32[64,1024]{1,0:T(8,128)S(1)}, u32[]{:S(2)}, u32[]{:S(2)}) collective-permute-start(f32[64,1024]{1,0:T(8,128)S(1)} %fusion.8), channel_id=1, source_target_pairs={{4,8},{5,9},{2,6},{3,7},{20,24},{21,25},{18,22},{19,23}} | collective-permute-start | bytes 786440 | tf_op jit(solution)/shard_map/ppermute | solution.py:255
  501.7 10.4 %collective-permute-start.22 = (f32[64,1024]{1,0:T(8,128)S(1)}, f32[64,1024]{1,0:T(8,128)S(1)}, u32[]{:S(2)}, u32[]{:S(2)}) collective-permute-start(f32[64,1024]{1,0:T(8,128)S(1)} %fusion.8), channel_id=1, source_target_pairs={{0,8},{1,9},{14,6},{15,7},{16,24},{17,25},{30,22},{31,23}} | collective-permute-start | bytes 786440 | tf_op jit(solution)/shard_map/ppermute | solution.py:255
  503.0 15.5 %collective-permute-start.23 = (f32[64,1024]{1,0:T(8,128)S(1)}, f32[64,1024]{1,0:T(8,128)S(1)}, u32[]{:S(2)}, u32[]{:S(2)}) collective-permute-start(f32[64,1024]{1,0:T(8,128)S(1)} %fusion.8), channel_id=1, source_target_pairs={{12,8},{13,9},{10,6},{11,7},{28,24},{29,25},{26,22},{27,23}} | collective-permute-start | bytes 786440 | tf_op jit(solution)/shard_map/ppermute | solution.py:255
  504.3 42.4 %collective-permute-start.24 = (bf16[2304,128]{1,0:T(8,128)(2,1)}, bf16[2304,128]{1,0:T(8,128)(2,1)}, u32[]{:S(2)}, u32[]{:S(2)}) collective-permute-start(bf16[2304,128]{1,0:T(8,128)(2,1)} %get-tuple-element.40), channel_id=1, source_target_pairs={{0,2},{2,0},{1,3},{3,1},{4,6},{6,4},{5,7},{7,5},{8,10},{10,8},{9,1... | collective-permute-start | bytes 1769480 | tf_op jit(solution)/shard_map/ppermute | solution.py:403
  550.0 2.8 collective-permute-start.26
  553.5 7.5 %collective-permute-start.27 = (bf16[64,1024]{1,0:T(8,128)(2,1)S(1)}, bf16[64,1024]{1,0:T(8,128)(2,1)S(1)}, u32[]{:S(2)}, u32[]{:S(2)}) collective-permute-start(bf16[64,1024]{1,0:T(8,128)(2,1)S(1)} %get-tuple-element.56), channel_id=1, source_target_pairs={{0,8},{1,9},{14,6},{15,7},{16,24},{17,25},{30,22},{31,23}} | collective-permute-start | bytes 393224 | tf_op jit(solution)/shard_map/ppermute | solution.py:277
  554.8 9.7 %collective-permute-start.28 = (bf16[64,1024]{1,0:T(8,128)(2,1)S(1)}, bf16[64,1024]{1,0:T(8,128)(2,1)S(1)}, u32[]{:S(2)}, u32[]{:S(2)}) collective-permute-start(bf16[64,1024]{1,0:T(8,128)(2,1)S(1)} %get-tuple-element.56), channel_id=1, source_target_pairs={{4,8},{5,9},{10,6},{11,7},{20,24},{21,25},{26,22},{27,23}} | collective-permute-start | bytes 393224 | tf_op jit(solution)/shard_map/ppermute | solution.py:277
  556.1 8.4 %collective-permute-start.29 = (bf16[64,1024]{1,0:T(8,128)(2,1)S(1)}, bf16[64,1024]{1,0:T(8,128)(2,1)S(1)}, u32[]{:S(2)}, u32[]{:S(2)}) collective-permute-start(bf16[64,1024]{1,0:T(8,128)(2,1)S(1)} %get-tuple-element.56), channel_id=1, source_target_pairs={{12,8},{13,9},{2,6},{3,7},{28,24},{29,25},{18,22},{19,23}} | collective-permute-start | bytes 393224 | tf_op jit(solution)/shard_map/ppermute | solution.py:277
  (7 other events, 19.6 us)

commit v4 on v3

--- a/solution.py
+++ b/solution.py
@@ -194,17 +194,16 @@
     out[...] = array_ref[...]
 
 
-def columns(array, at, width):
-    step = array.shape[0] // 2
+def columns(array, at, width, first, steps, height):
     return pl.pallas_call(
         copy_kernel,
         grid_spec=pltpu.PrefetchScalarGridSpec(
             num_scalar_prefetch=1,
-            grid=(2,),
-            in_specs=[pl.BlockSpec((step, width), lambda i, at_ref: (i, at_ref[0]))],
-            out_specs=pl.BlockSpec((step, width), lambda i, at_ref: (i, 0)),
+            grid=(steps,),
+            in_specs=[pl.BlockSpec((height, width), lambda i, at_ref: (i + first, at_ref[0]))],
+            out_specs=pl.BlockSpec((height, width), lambda i, at_ref: (i, 0)),
         ),
-        out_shape=jax.ShapeDtypeStruct((array.shape[0], width), array.dtype),
+        out_shape=jax.ShapeDtypeStruct((steps * height, width), array.dtype),
         compiler_params=pltpu.CompilerParams(vmem_limit_bytes=VMEM),
         cost_estimate=SMALL,
     )(at[None], array)
@@ -310,8 +309,14 @@
     none = jnp.zeros((1,), jnp.int32)
     raws = min(2, chunks)
     width = BAND * size
-    first = columns(eig_lower, turn // (raws * LANES), raws * LANES)
-    behind, first = lax.optimization_barrier((eig_lower, first))
+    sixth = depth // 6
+    at = turn // (raws * LANES)
+    head = columns(eig_lower, at, raws * LANES, 0, 1, sixth)
+    behind, head = lax.optimization_barrier((eig_lower, head))
+    first = columns(behind, at, raws * LANES, 1, 5, sixth)
+    over = lambda array, step: lax.ppermute(array, "win", [(i, (i + step) % wins) for i in range(wins)])
+    heads = [over(head, step) for step in range(1, wins)]
+    behind, heads[:1] = lax.optimization_barrier((behind, heads[:1]))
     low, high = halo(behind[-width:], behind[:width], owners)
 
     tail = LANES // 2 if wins == 2 and reps == 2 and share == 2 * LANES else 0
@@ -363,6 +368,7 @@
                 late.extend(to_chip(part, chip))
             return part
         if kind == "raw":
+            piece = jnp.concatenate([heads[step - 1], piece], axis=0)
             ends = halo(piece[-width:], piece[:width], owners)
             (piece,) = image(where_at, block_count, none, dipole, piece, *ends, ())
         part = product(piece, eig_upper)
@@ -400,7 +406,7 @@
             if ready >= 0:
                 needs = got[ready] if transfers[ready][1] == "cut" else (got[ready], made)
                 array, _ = lax.optimization_barrier((array, needs))
-            got.append(lax.ppermute(array, "win", [(i, (i + step) % wins) for i in range(wins)]))
+            got.append(over(array, step))
     if not tail:
         return tuple(lines(moments_of(0, share), [], 0, share, [], *levels))
     return tuple(lines(rest, late, LANES, LANES, outs, *levels))

time: 572 us -> 570 us (level)
  waiting for transfers between devices: 251 us -> 233 us
  other arithmetic: 15.2 us -> 24 us
  Pallas kernels: 222 us -> 228 us
    ppermute x6 -> x7, waiting for transfers between devices: 72.6 us -> 60.1 us  [shards(): lax.ppermute(array, 'win', [(i, (i + step) % wins) for i in range(wins)])]
    concatenate x0 -> x1, other arithmetic: none -> 8.74 us  [work(): piece = jnp.concatenate([heads[step - 1], piece], axis=0)]
  transfers between devices with their start and end apart: 30 -> 31, of which waited for: 22 -> 21; matrix products, arithmetic and copies ran while one was open for 6% -> 8% of each run, Pallas kernels for 38% -> 39%
where the time goes in v4:
time: 570 us; the launch traced here: 566 us
  waiting for transfers between devices  233 us (41%)
  Pallas kernels  228 us (40%)
  starting transfers between devices  54.3 us (10%)
  other arithmetic  24 us (4%)
  local copies, waits for them, and re-layouts  13.1 us (2%)
  matrix products  12.4 us (2%)
    ppermute x12, waiting for transfers between devices, to_chips(): terms.append(lax.ppermute(piece, AXES, pairs))  137 us
    pallas_call x2, Pallas kernels, image(): pl.pallas_call(functools.partial(image_kernel, slots, pieces), grid_spec=...  112 us
    pallas_call x5, Pallas kernels, product(): pl.pallas_call(product_kernel, grid=(depth // step,), in_specs=[pl.BlockS...  101 us
    ppermute x7, waiting for transfers between devices, shards(): lax.ppermute(array, 'win', [(i, (i + step) % wins) for i in range(wins)])  60.1 us
    ppermute x12, starting transfers between devices, to_chips(): terms.append(lax.ppermute(piece, AXES, pairs))  21.5 us
    ppermute x2, waiting for transfers between devices, halo(): low = lax.ppermute(last, axes, up)  20.5 us
    dot_general x2, matrix products, part_product(): lax.dot_general(chunk, eig_upper[first:first + chunk.shape[0]], (((0,), (...  12.4 us
  transfers between devices with their start and end apart: 31, of which 21 were waited for; matrix products, arithmetic and copies ran while one was open for 8% of the time, Pallas kernels for 39%

profile of v4, /device:TPU:11, one launch (start us, length us, event | category | flops | bytes accessed | tf_op | source)
XLA Modules:
  0.0 566.0 jit_solution(7959187016118084339)
XLA Ops:
  3.2 6.5 %shard_map.107 = bf16[10240,256]{1,0:T(8,128)(2,1)} custom-call(s32[1]{0:T(128)} %bitcast.5.at_ref, bf16[12288,1024]{1,0:T(8,128)(2,1)} %array_ref.2), custom_call_target="tpu_custom_call" | custom-call | flops 1024 | bytes 1024 | tf_op jit(solution)/shard_map/pallas_call | solution.py:198
  10.9 16.2 %collective-permute-done = bf16[2048,256]{1,0:T(8,128)(2,1)S(1)} collective-permute-done((bf16[2048,256]{1,0:T(8,128)(2,1)}, bf16[2048,256]{1,0:T(8,128)(2,1)S(1)}, u32[]{:S(2)}, u32[]{:S(2)}) %collective-permute-start) | collective-permute-done | bytes 1048608 | tf_op jit(solution)/shard_map/ppermute | solution.py:317
  27.2 4.6 fusion.9
  31.8 5.8 %collective-permute-start.1 = (bf16[1024,1024]{1,0:T(8,128)(2,1)}, bf16[1024,1024]{1,0:T(8,128)(2,1)S(1)}, u32[]{:S(2)}, u32[]{:S(2)}) collective-permute-start(bf16[1024,1024]{1,0:T(8,128)(2,1)} %get-tuple-element.53), channel_id=1, source_target_pairs={{0,1},{1,4},{4,5},{5,8},{8,9},{9,12},{12,13},{2,3},{3,6},{6,7},{7,... | collective-permute-start | bytes 6291464 | tf_op jit(solution)/shard_map/ppermute | solution.py:218
  40.3 20.5 %collective-permute-done.1.refs_2_.refs_5_ = bf16[1024,1024]{1,0:T(8,128)(2,1)S(1)} collective-permute-done((bf16[1024,1024]{1,0:T(8,128)(2,1)}, bf16[1024,1024]{1,0:T(8,128)(2,1)S(1)}, u32[]{:S(2)}, u32[]{:S(2)}) %collective-permute-start.1) | collective-permute-done | bytes 2097184 | tf_op jit(solution)/shard_map/ppermute | solution.py:218
  60.9 4.7 collective-permute-done.2.refs_3_.refs_6_
  65.5 70.9 %shard_map.105 = (bf16[12288,1024]{1,0:T(8,128)(2,1)}, bf16[12288,256]{1,0:T(8,128)(2,1)}, bf16[12288,256]{1,0:T(8,128)(2,1)}, bf16[12288,128]{1,0:T(8,128)(2,1)...) custom-call(s32[144]{0:T(256)} %reshape.30.where_ref, s32[48]{0:T(128)} %count_ref.3, s32[1]{0:T(128)} %bitcast.4.turn_ref, ...), custom_call_target="tpu_custom_call" | custom-call | flops 1024 | bytes 1024 | tf_op jit(solution)/shard_map/pallas_call | solution.py:95
  136.8 4.1 collective-permute-start.10
  140.9 33.1 %shard_map.106 = f32[1024,1024]{1,0:T(8,128)} custom-call(bf16[12288,1024]{1,0:T(8,128)(2,1)} %get-tuple-element.29.chunk_ref, bf16[12288,1024]{1,0:T(8,128)(2,1)} %upper_ref.9), custom_call_target="tpu_custom_call" | custom-call | flops 1024 | bytes 1024 | tf_op jit(solution)/shard_map/pallas_call | solution.py:126
  177.8 8.7 %pad_maximum_fusion.refs_0_.refs_1_.refs_4_ = bf16[12288,256]{1,0:T(8,128)(2,1)} fusion(bf16[10240,256]{1,0:T(8,128)(2,1)} %collective-permute-done.8, bf16[2048,256]{1,0:T(8,128)(2,1)S(1)} %collective-permute-done), kind=kLoop, calls=%fused_computation.2 | loop fusion | flops 12582912 | bytes 12582912 | tf_op jit(solution)/shard_map/concatenate | solution.py:371
  188.1 40.9 %shard_map.108.chunk_ref = bf16[12288,256]{1,0:T(8,128)(2,1)} custom-call(s32[144]{0:T(256)} %reshape.30.where_ref, s32[48]{0:T(128)} %count_ref.3, s32[1]{0:T(128)} %constant.188.clone.1.turn_ref, bf16[48,3,256,256]{3,2,1,0:T(8,128)(2,1)} %dipole_ref.3, bf16[12288,256]{1,0:T(8,128)(2,1)} %pad_maximum_fusion.refs_0_.refs_1_.refs_4_, ...), custom_call_target="tpu_custom_call" | custom-call | flops 1024 | bytes 1024 | tf_op jit(solution)/shard_map/pallas_call | solution.py:95
  229.0 17.7 %shard_map.109 = f32[256,1024]{1,0:T(8,128)} custom-call(bf16[12288,256]{1,0:T(8,128)(2,1)} %shard_map.108.chunk_ref, bf16[12288,1024]{1,0:T(8,128)(2,1)} %upper_ref.9), custom_call_target="tpu_custom_call" | custom-call | flops 1024 | bytes 1024 | tf_op jit(solution)/shard_map/pallas_call | solution.py:126
  252.1 22.3 %collective-permute-done.7.chunk_ref = bf16[12288,256]{1,0:T(8,128)(2,1)} collective-permute-done((bf16[12288,256]{1,0:T(8,128)(2,1)}, bf16[12288,256]{1,0:T(8,128)(2,1)}, u32[]{:S(2)}, u32[]{:S(2)}) %collective-permute-start.7) | collective-permute-done | bytes 6291488 | tf_op jit(solution)/shard_map/ppermute | solution.py:317
  274.5 17.7 %shard_map.110 = f32[256,1024]{1,0:T(8,128)} custom-call(bf16[12288,256]{1,0:T(8,128)(2,1)} %collective-permute-done.7.chunk_ref, bf16[12288,1024]{1,0:T(8,128)(2,1)} %upper_ref.9), custom_call_target="tpu_custom_call" | custom-call | flops 1024 | bytes 1024 | tf_op jit(solution)/shard_map/pallas_call | solution.py:126
  298.8 4.2 collective-permute-start.4
  309.7 58.9 %collective-permute-done.4 = f32[256,1024]{1,0:T(8,128)} collective-permute-done((f32[256,1024]{1,0:T(8,128)S(1)}, f32[256,1024]{1,0:T(8,128)}, u32[]{:S(2)}, u32[]{:S(2)}) %collective-permute-start.4) | collective-permute-done | bytes 1048608 | tf_op jit(solution)/shard_map/ppermute | solution.py:254
  370.3 20.8 %collective-permute-done.5 = f32[256,1024]{1,0:T(8,128)} collective-permute-done((f32[256,1024]{1,0:T(8,128)S(1)}, f32[256,1024]{1,0:T(8,128)}, u32[]{:S(2)}, u32[]{:S(2)}) %collective-permute-start.5) | collective-permute-done | bytes 1048608 | tf_op jit(solution)/shard_map/ppermute | solution.py:254
  396.1 21.5 %collective-permute-done.14 = f32[256,1024]{1,0:T(8,128)} collective-permute-done((f32[256,1024]{1,0:T(8,128)}, f32[256,1024]{1,0:T(8,128)}, u32[]{:S(2)}, u32[]{:S(2)}) %collective-permute-start.14) | collective-permute-done | bytes 1048608 | tf_op jit(solution)/shard_map/ppermute | solution.py:254
  419.8 17.7 %shard_map.111 = f32[256,1024]{1,0:T(8,128)} custom-call(bf16[12288,256]{1,0:T(8,128)(2,1)} %collective-permute-done.16.chunk_ref, bf16[12288,1024]{1,0:T(8,128)(2,1)} %upper_ref.9), custom_call_target="tpu_custom_call" | custom-call | flops 1024 | bytes 1024 | tf_op jit(solution)/shard_map/pallas_call | solution.py:126
  445.7 12.0 %collective-permute-done.18 = f32[128,1024]{1,0:T(8,128)S(1)} collective-permute-done((f32[128,1024]{1,0:T(8,128)S(1)}, f32[128,1024]{1,0:T(8,128)S(1)}, u32[]{:S(2)}, u32[]{:S(2)}) %collective-permute-start.18) | collective-permute-done | bytes 524320 | tf_op jit(solution)/shard_map/ppermute | solution.py:254
  459.2 11.9 %collective-permute-done.20 = f32[128,1024]{1,0:T(8,128)} collective-permute-done((f32[128,1024]{1,0:T(8,128)S(1)}, f32[128,1024]{1,0:T(8,128)}, u32[]{:S(2)}, u32[]{:S(2)}) %collective-permute-start.20) | collective-permute-done | bytes 524320 | tf_op jit(solution)/shard_map/ppermute | solution.py:254
  473.4 3.3 collective-permute-done.15.chunk_ref
  476.7 15.3 %shard_map.112 = f32[128,1024]{1,0:T(8,128)} custom-call(bf16[12288,128]{1,0:T(8,128)(2,1)} %collective-permute-done.15.chunk_ref, bf16[12288,1024]{1,0:T(8,128)(2,1)} %upper_ref.9), custom_call_target="tpu_custom_call" | custom-call | flops 1024 | bytes 1024 | tf_op jit(solution)/shard_map/pallas_call | solution.py:126
  502.8 3.0 shard_map.113
  509.5 6.4 %collective-permute-done.24 = f32[64,1024]{1,0:T(8,128)S(1)} collective-permute-done((f32[64,1024]{1,0:T(8,128)S(1)}, f32[64,1024]{1,0:T(8,128)S(1)}, u32[]{:S(2)}, u32[]{:S(2)}) %collective-permute-start.24) | collective-permute-done | bytes 262176 | tf_op jit(solution)/shard_map/ppermute | solution.py:254
  516.8 14.6 %collective-permute-done.26 = bf16[9984,128]{1,0:T(8,128)(2,1)} collective-permute-done((bf16[9984,128]{1,0:T(8,128)(2,1)}, bf16[9984,128]{1,0:T(8,128)(2,1)}, u32[]{:S(2)}, u32[]{:S(2)}) %collective-permute-start.26) | collective-permute-done | bytes 2555936 | tf_op jit(solution)/shard_map/ppermute | solution.py:317
  531.5 9.1 %fusion = f32[128,1024]{1,0:T(8,128)S(1)} fusion(bf16[9984,128]{1,0:T(8,128)(2,1)} %collective-permute-done.26, bf16[12288,1024]{1,0:T(8,128)(2,1)} %upper_ref.9), kind=kOutput, calls=%fused_computation | convolution fusion | flops 2617245696 | bytes 23527424 | tf_op jit(solution)/shard_map/dot_general | solution.py:138
  540.6 3.5 collective-permute-done.25
  544.1 3.3 fusion.2
  554.9 3.6 collective-permute-done.28.refs_2_
  558.6 3.5 collective-permute-done.29.refs_3_
  562.8 3.3 shard_map.114
  (86 shorter events, 75.3 us)
Async XLA Ops:
  2.9 24.2 %collective-permute-start = (bf16[2048,256]{1,0:T(8,128)(2,1)}, bf16[2048,256]{1,0:T(8,128)(2,1)S(1)}, u32[]{:S(2)}, u32[]{:S(2)}) collective-permute-start(bf16[2048,256]{1,0:T(8,128)(2,1)} %shard_map.104), channel_id=1, source_target_pairs={{0,2},{2,0},{1,3},{3,1},{4,6},{6,4},{5,7},{7,5},{8,10},{10,8},{9,1... | collective-permute-start | bytes 3145736 | tf_op jit(solution)/shard_map/ppermute | solution.py:317
  9.7 164.3 %collective-permute-start.8 = (bf16[10240,256]{1,0:T(8,128)(2,1)}, bf16[10240,256]{1,0:T(8,128)(2,1)}, u32[]{:S(2)}, u32[]{:S(2)}) collective-permute-start(bf16[10240,256]{1,0:T(8,128)(2,1)} %shard_map.107), channel_id=1, source_target_pairs={{0,2},{2,0},{1,3},{3,1},{4,6},{6,4},{5,7},{7,5},{8,10},{10,8},{9,1... | collective-permute-start | bytes 15728648 | tf_op jit(solution)/shard_map/ppermute | solution.py:317
  31.8 29.1 %collective-permute-start.1 = (bf16[1024,1024]{1,0:T(8,128)(2,1)}, bf16[1024,1024]{1,0:T(8,128)(2,1)S(1)}, u32[]{:S(2)}, u32[]{:S(2)}) collective-permute-start(bf16[1024,1024]{1,0:T(8,128)(2,1)} %get-tuple-element.53), channel_id=1, source_target_pairs={{0,1},{1,4},{4,5},{5,8},{8,9},{9,12},{12,13},{2,3},{3,6},{6,7},{7,... | collective-permute-start | bytes 6291464 | tf_op jit(solution)/shard_map/ppermute | solution.py:218
  37.6 28.0 %collective-permute-start.2 = (bf16[1024,1024]{1,0:T(8,128)(2,1)}, bf16[1024,1024]{1,0:T(8,128)(2,1)}, u32[]{:S(2)}, u32[]{:S(2)}) collective-permute-start(bf16[1024,1024]{1,0:T(8,128)(2,1)} %get-tuple-element.52), channel_id=1, source_target_pairs={{1,0},{4,1},{5,4},{8,5},{9,8},{12,9},{13,12},{3,2},{6,3},{7,6},{10... | collective-permute-start | bytes 6291464 | tf_op jit(solution)/shard_map/ppermute | solution.py:219
  136.4 138.0 %collective-permute-start.7 = (bf16[12288,256]{1,0:T(8,128)(2,1)}, bf16[12288,256]{1,0:T(8,128)(2,1)}, u32[]{:S(2)}, u32[]{:S(2)}) collective-permute-start(bf16[12288,256]{1,0:T(8,128)(2,1)} %get-tuple-element.30), channel_id=1, source_target_pairs={{0,2},{2,0},{1,3},{3,1},{4,6},{6,4},{5,7},{7,5},{8,10},{10,8},{9,1... | collective-permute-start | bytes 18874376 | tf_op jit(solution)/shard_map/ppermute | solution.py:317
  136.8 49.7 %collective-permute-start.10 = (bf16[1024,256]{1,0:T(8,128)(2,1)S(1)}, bf16[1024,256]{1,0:T(8,128)(2,1)S(1)}, u32[]{:S(2)}, u32[]{:S(2)}) collective-permute-start(bf16[1024,256]{1,0:T(8,128)(2,1)S(1)} %slice.34), channel_id=1, source_target_pairs={{1,0},{4,1},{5,4},{8,5},{9,8},{12,9},{13,12},{3,2},{6,3},{7,6},{10... | collective-permute-start | bytes 1572872 | tf_op jit(solution)/shard_map/ppermute | solution.py:219
  175.1 11.4 %collective-permute-start.9 = (bf16[1024,256]{1,0:T(8,128)(2,1)S(1)}, bf16[1024,256]{1,0:T(8,128)(2,1)S(1)}, u32[]{:S(2)}, u32[]{:S(2)}) collective-permute-start(bf16[1024,256]{1,0:T(8,128)(2,1)S(1)} %slice.33), channel_id=1, source_target_pairs={{0,1},{1,4},{4,5},{5,8},{8,9},{9,12},{12,13},{2,3},{3,6},{6,7},{7,... | collective-permute-start | bytes 1572872 | tf_op jit(solution)/shard_map/ppermute | solution.py:218
  246.7 173.2 %collective-permute-start.16 = (bf16[12288,256]{1,0:T(8,128)(2,1)}, bf16[12288,256]{1,0:T(8,128)(2,1)}, u32[]{:S(2)}, u32[]{:S(2)}) collective-permute-start(bf16[12288,256]{1,0:T(8,128)(2,1)} %get-tuple-element.38), channel_id=1, source_target_pairs={{0,2},{2,0},{1,3},{3,1},{4,6},{6,4},{5,7},{7,5},{8,10},{10,8},{9,1... | collective-permute-start | bytes 18874376 | tf_op jit(solution)/shard_map/ppermute | solution.py:317
  249.7 46.8 %collective-permute-start.3 = (f32[2,256,1024]{2,1,0:T(8,128)S(1)}, f32[2,256,1024]{2,1,0:T(8,128)}, u32[]{:S(2)}, u32[]{:S(2)}) collective-permute-start(f32[2,256,1024]{2,1,0:T(8,128)S(1)} %dynamic-slice_bitcast_fusion), channel_id=1, source_target_pairs={{0,1},{1,0},{2,3},{3,2},{4,5},{5,4},{6,7},{7,6},{8,9},{9,8},{10,11... | collective-permute-start | bytes 6291464 | tf_op jit(solution)/shard_map/ppermute | solution.py:234
  252.1 40.0 %copy-start.2 = (f32[256,1024]{1,0:T(8,128)S(1)}, f32[256,1024]{1,0:T(8,128)}, u32[]{:S(2)}) copy-start(f32[256,1024]{1,0:T(8,128)} %shard_map.109) | copy-start | bytes 3145732
  293.8 13.2 %collective-permute-start.11 = (f32[1,256,1024]{2,1,0:T(8,128)S(1)}, f32[1,256,1024]{2,1,0:T(8,128)S(1)}, u32[]{:S(2)}, u32[]{:S(2)}) collective-permute-start(f32[1,256,1024]{2,1,0:T(8,128)S(1)} %dynamic-slice_bitcast_fusion.1), channel_id=1, source_target_pairs={{0,1},{1,0},{2,3},{3,2},{4,5},{5,4},{6,7},{7,6},{8,9},{9,8},{10,11... | collective-permute-start | bytes 3145736 | tf_op jit(solution)/shard_map/ppermute | solution.py:234
  298.8 69.8 %collective-permute-start.4 = (f32[256,1024]{1,0:T(8,128)S(1)}, f32[256,1024]{1,0:T(8,128)}, u32[]{:S(2)}, u32[]{:S(2)}) collective-permute-start(f32[256,1024]{1,0:T(8,128)S(1)} %get-tuple-element.56), channel_id=1, source_target_pairs={{12,0},{13,1},{0,4},{1,5},{6,10},{7,11},{10,14},{11,15},{28,16},{2... | collective-permute-start | bytes 3145736 | tf_op jit(solution)/shard_map/ppermute | solution.py:254
  302.9 88.1 %collective-permute-start.5 = (f32[256,1024]{1,0:T(8,128)S(1)}, f32[256,1024]{1,0:T(8,128)}, u32[]{:S(2)}, u32[]{:S(2)}) collective-permute-start(f32[256,1024]{1,0:T(8,128)S(1)} %get-tuple-element.54), channel_id=1, source_target_pairs={{8,0},{9,1},{12,4},{13,5},{2,10},{3,11},{6,14},{7,15},{24,16},{25,... | collective-permute-start | bytes 3145736 | tf_op jit(solution)/shard_map/ppermute | solution.py:254
  305.3 88.0 %collective-permute-start.6 = (f32[256,1024]{1,0:T(8,128)S(1)}, f32[256,1024]{1,0:T(8,128)}, u32[]{:S(2)}, u32[]{:S(2)}) collective-permute-start(f32[256,1024]{1,0:T(8,128)S(1)} %get-tuple-element.55), channel_id=1, source_target_pairs={{4,0},{5,1},{8,4},{9,5},{14,10},{15,11},{2,14},{3,15},{20,16},{21,... | collective-permute-start | bytes 3145736 | tf_op jit(solution)/shard_map/ppermute | solution.py:254
  308.0 88.0 %collective-permute-start.12 = (f32[256,1024]{1,0:T(8,128)}, f32[256,1024]{1,0:T(8,128)}, u32[]{:S(2)}, u32[]{:S(2)}) collective-permute-start(f32[256,1024]{1,0:T(8,128)} %fusion.4), channel_id=1, source_target_pairs={{8,12},{9,13},{14,2},{15,3},{24,28},{25,29},{30,18},{31,19}} | collective-permute-start | bytes 3145736 | tf_op jit(solution)/shard_map/ppermute | solution.py:254
  368.6 27.5 %collective-permute-start.13 = (f32[256,1024]{1,0:T(8,128)}, f32[256,1024]{1,0:T(8,128)}, u32[]{:S(2)}, u32[]{:S(2)}) collective-permute-start(f32[256,1024]{1,0:T(8,128)} %fusion.4), channel_id=1, source_target_pairs={{4,12},{5,13},{10,2},{11,3},{20,28},{21,29},{26,18},{27,19}} | collective-permute-start | bytes 3145736 | tf_op jit(solution)/shard_map/ppermute | solution.py:254
  391.1 26.5 %collective-permute-start.14 = (f32[256,1024]{1,0:T(8,128)}, f32[256,1024]{1,0:T(8,128)}, u32[]{:S(2)}, u32[]{:S(2)}) collective-permute-start(f32[256,1024]{1,0:T(8,128)} %fusion.4), channel_id=1, source_target_pairs={{0,12},{1,13},{6,2},{7,3},{16,28},{17,29},{22,18},{23,19}} | collective-permute-start | bytes 3145736 | tf_op jit(solution)/shard_map/ppermute | solution.py:254
  393.3 83.4 %collective-permute-start.15 = (bf16[12288,128]{1,0:T(8,128)(2,1)}, bf16[12288,128]{1,0:T(8,128)(2,1)}, u32[]{:S(2)}, u32[]{:S(2)}) collective-permute-start(bf16[12288,128]{1,0:T(8,128)(2,1)} %get-tuple-element.36), channel_id=1, source_target_pairs={{0,2},{2,0},{1,3},{3,1},{4,6},{6,4},{5,7},{7,5},{8,10},{10,8},{9,1... | collective-permute-start | bytes 9437192 | tf_op jit(solution)/shard_map/ppermute | solution.py:317
  438.6 2.1 collective-permute-start.17
  439.2 92.3 %collective-permute-start.26 = (bf16[9984,128]{1,0:T(8,128)(2,1)}, bf16[9984,128]{1,0:T(8,128)(2,1)}, u32[]{:S(2)}, u32[]{:S(2)}) collective-permute-start(bf16[9984,128]{1,0:T(8,128)(2,1)} %get-tuple-element.46), channel_id=1, source_target_pairs={{0,2},{2,0},{1,3},{3,1},{4,6},{6,4},{5,7},{7,5},{8,10},{10,8},{9,1... | collective-permute-start | bytes 7667720 | tf_op jit(solution)/shard_map/ppermute | solution.py:317
  441.8 15.9 %collective-permute-start.18 = (f32[128,1024]{1,0:T(8,128)S(1)}, f32[128,1024]{1,0:T(8,128)S(1)}, u32[]{:S(2)}, u32[]{:S(2)}) collective-permute-start(f32[128,1024]{1,0:T(8,128)S(1)} %fusion.7), channel_id=1, source_target_pairs={{4,8},{5,9},{2,6},{3,7},{20,24},{21,25},{18,22},{19,23}} | collective-permute-start | bytes 1572872 | tf_op jit(solution)/shard_map/ppermute | solution.py:254
  443.1 16.1 %collective-permute-start.19 = (f32[128,1024]{1,0:T(8,128)S(1)}, f32[128,1024]{1,0:T(8,128)}, u32[]{:S(2)}, u32[]{:S(2)}) collective-permute-start(f32[128,1024]{1,0:T(8,128)S(1)} %fusion.7), channel_id=1, source_target_pairs={{0,8},{1,9},{14,6},{15,7},{16,24},{17,25},{30,22},{31,23}} | collective-permute-start | bytes 1572872 | tf_op jit(solution)/shard_map/ppermute | solution.py:254
  444.4 26.7 %collective-permute-start.20 = (f32[128,1024]{1,0:T(8,128)S(1)}, f32[128,1024]{1,0:T(8,128)}, u32[]{:S(2)}, u32[]{:S(2)}) collective-permute-start(f32[128,1024]{1,0:T(8,128)S(1)} %fusion.7), channel_id=1, source_target_pairs={{12,8},{13,9},{10,6},{11,7},{28,24},{29,25},{26,22},{27,23}} | collective-permute-start | bytes 1572872 | tf_op jit(solution)/shard_map/ppermute | solution.py:254
  493.0 3.9 collective-permute-start.21
  497.8 9.5 %collective-permute-start.22 = (f32[64,1024]{1,0:T(8,128)S(1)}, f32[64,1024]{1,0:T(8,128)S(1)}, u32[]{:S(2)}, u32[]{:S(2)}) collective-permute-start(f32[64,1024]{1,0:T(8,128)S(1)} %fusion.8), channel_id=1, source_target_pairs={{4,8},{5,9},{2,6},{3,7},{20,24},{21,25},{18,22},{19,23}} | collective-permute-start | bytes 786440 | tf_op jit(solution)/shard_map/ppermute | solution.py:254
  499.1 10.4 %collective-permute-start.23 = (f32[64,1024]{1,0:T(8,128)S(1)}, f32[64,1024]{1,0:T(8,128)S(1)}, u32[]{:S(2)}, u32[]{:S(2)}) collective-permute-start(f32[64,1024]{1,0:T(8,128)S(1)} %fusion.8), channel_id=1, source_target_pairs={{0,8},{1,9},{14,6},{15,7},{16,24},{17,25},{30,22},{31,23}} | collective-permute-start | bytes 786440 | tf_op jit(solution)/shard_map/ppermute | solution.py:254
  500.4 15.5 %collective-permute-start.24 = (f32[64,1024]{1,0:T(8,128)S(1)}, f32[64,1024]{1,0:T(8,128)S(1)}, u32[]{:S(2)}, u32[]{:S(2)}) collective-permute-start(f32[64,1024]{1,0:T(8,128)S(1)} %fusion.8), channel_id=1, source_target_pairs={{12,8},{13,9},{10,6},{11,7},{28,24},{29,25},{26,22},{27,23}} | collective-permute-start | bytes 786440 | tf_op jit(solution)/shard_map/ppermute | solution.py:254
  501.7 42.4 %collective-permute-start.25 = (bf16[2304,128]{1,0:T(8,128)(2,1)}, bf16[2304,128]{1,0:T(8,128)(2,1)}, u32[]{:S(2)}, u32[]{:S(2)}) collective-permute-start(bf16[2304,128]{1,0:T(8,128)(2,1)} %get-tuple-element.44), channel_id=1, source_target_pairs={{0,2},{2,0},{1,3},{3,1},{4,6},{6,4},{5,7},{7,5},{8,10},{10,8},{9,1... | collective-permute-start | bytes 1769480 | tf_op jit(solution)/shard_map/ppermute | solution.py:317
  547.5 2.8 collective-permute-start.27
  551.1 7.5 %collective-permute-start.28 = (bf16[64,1024]{1,0:T(8,128)(2,1)S(1)}, bf16[64,1024]{1,0:T(8,128)(2,1)S(1)}, u32[]{:S(2)}, u32[]{:S(2)}) collective-permute-start(bf16[64,1024]{1,0:T(8,128)(2,1)S(1)} %get-tuple-element.58), channel_id=1, source_target_pairs={{0,8},{1,9},{14,6},{15,7},{16,24},{17,25},{30,22},{31,23}} | collective-permute-start | bytes 393224 | tf_op jit(solution)/shard_map/ppermute | solution.py:276
  552.3 9.7 %collective-permute-start.29 = (bf16[64,1024]{1,0:T(8,128)(2,1)S(1)}, bf16[64,1024]{1,0:T(8,128)(2,1)S(1)}, u32[]{:S(2)}, u32[]{:S(2)}) collective-permute-start(bf16[64,1024]{1,0:T(8,128)(2,1)S(1)} %get-tuple-element.58), channel_id=1, source_target_pairs={{4,8},{5,9},{10,6},{11,7},{20,24},{21,25},{26,22},{27,23}} | collective-permute-start | bytes 393224 | tf_op jit(solution)/shard_map/ppermute | solution.py:276
  553.6 8.4 %collective-permute-start.30 = (bf16[64,1024]{1,0:T(8,128)(2,1)S(1)}, bf16[64,1024]{1,0:T(8,128)(2,1)S(1)}, u32[]{:S(2)}, u32[]{:S(2)}) collective-permute-start(bf16[64,1024]{1,0:T(8,128)(2,1)S(1)} %get-tuple-element.58), channel_id=1, source_target_pairs={{12,8},{13,9},{2,6},{3,7},{28,24},{29,25},{18,22},{19,23}} | collective-permute-start | bytes 393224 | tf_op jit(solution)/shard_map/ppermute | solution.py:276
  (8 other events, 45.3 us)
